TPU v7x, 512 devices: a whole 4x4x16 slice. The times are simulated.
512 devices in a mesh: section: 16 (over z), expert: 32 (over y, x, core).
Axes of the slice: x: 4, y: 4, z: 16, core: 2. Of those that a mesh axis runs over, the one named last changes fastest.
Arguments:
- tokens: bfloat16 [8, 256, 2048], P(None, 'expert', 'section'), may hold values from -6 to 6
- norm_gain: float32 [16, 2048], P('section'), may hold values from 0.1 to 1.9
- gate_weight: bfloat16 [16, 32, 2048, 384], P('section', 'expert'), may hold values from -0.125 to 0.125
- up_weight: bfloat16 [16, 32, 2048, 384], P('section', 'expert'), may hold values from -0.125 to 0.125
- down_weight: bfloat16 [16, 32, 384, 2048], P('section', 'expert'), may hold values from -0.3125 to 0.3125
- expert_ids: int32 [16, 8, 256, 8], P('section', None, 'expert'), may hold values from 0 to 31, all different within a row; in each aligned block of 8 rows (0 to 7, 8 to 15, ..., all dimensions but the last counted through in order) at most 2 rows name the same one
- gate_probs: float32 [16, 8, 256, 8], P('section', None, 'expert'), may hold values from 0.05 to 1
Outputs:
- hidden_states: bfloat16 [16, 8, 256, 2048], P('section', None, 'expert')
Inputs may be any that keep to these rules, and one draw needn't show every extreme that they name: `expert_ids`: in the 8 rows of one index of expert for one layer and micro-batch (aligned blocks of 8 rows), no expert is named by more than 2 rows, a bound that some block reaches in every draw.
All inputs are finite; a program needn't handle non-finite values.
Results may differ from a plain program's by a relative error of at most 0.04.
Values may be sent and summed in bfloat16 or wider, within the bound.
No kernel may reach another device: no remote copies, remote signals or barrier semaphores. Data moves between devices by JAX's collectives and lax.ppermute only.
A program may use at most 64 MiB of HBM per device.

v0:
```python
import jax
import jax.numpy as jnp
from jax import lax
from jax.sharding import PartitionSpec as P

CAP = 2


EPS = 1e-06


def passed_along(value, axis, by):
    length = lax.axis_size(axis)
    pairs = [(i, i + by) for i in range(length) if 0 <= i + by < length]
    return lax.ppermute(value, axis, pairs)


def expert_block(routed, w_gate, w_up, w_down):
    gate_proj = jnp.einsum("escd,edf->escf", routed, w_gate, preferred_element_type=jnp.float32)
    up_proj = jnp.einsum("escd,edf->escf", routed, w_up, preferred_element_type=jnp.float32)
    active = (jax.nn.silu(gate_proj) * up_proj).astype(jnp.bfloat16)
    return jnp.einsum("escf,efd->escd", active, w_down, preferred_element_type=jnp.float32).astype(
        jnp.bfloat16
    )


def slot_numbers(flat_ids, experts, capacity):
    onehot = (flat_ids[..., None] == jnp.arange(experts, dtype=jnp.int32)).astype(jnp.int32)
    before = jnp.cumsum(onehot, axis=-2) - onehot
    return flat_ids * capacity + jnp.sum(onehot * before, axis=-1)


def moe_layer(layer_input, norm_scale, expert_list, gate_share, w_gate, w_up, w_down):
    row_count, columns = layer_input.shape
    top_count = expert_list.shape[1]
    experts_local = w_gate.shape[0]
    groups = lax.axis_size("expert")
    experts = experts_local * groups
    capacity = CAP
    widened = layer_input.astype(jnp.float32)
    normed = (
        widened * lax.rsqrt(jnp.mean(widened * widened, axis=-1, keepdims=True) + EPS) * norm_scale
    ).astype(jnp.bfloat16)
    weight = gate_share / jnp.sum(gate_share, axis=-1, keepdims=True)
    slot_index = slot_numbers(
        expert_list.reshape(row_count * top_count), experts, capacity
    ).reshape(row_count, top_count)
    target = jnp.arange(experts * capacity, dtype=jnp.int32)
    placement = jnp.sum(
        (slot_index[None, :, :] == target[:, None, None]).astype(jnp.bfloat16), axis=2
    )
    sending = jnp.dot(placement, normed, preferred_element_type=jnp.float32).astype(jnp.bfloat16)
    sending = sending.reshape(experts, 1, capacity, columns)
    results = expert_block(
        lax.all_to_all(sending, "expert", split_axis=0, concat_axis=1, tiled=True),
        w_gate,
        w_up,
        w_down,
    )
    returned = lax.all_to_all(results, "expert", split_axis=1, concat_axis=0, tiled=True)
    returns_wide = returned.reshape(experts * capacity, columns).astype(jnp.float32)
    mixing = jnp.sum(
        (slot_index[:, :, None] == target[None, None, :]).astype(jnp.float32) * weight[:, :, None],
        axis=1,
    )
    mixed = jnp.dot(mixing, returns_wide, precision=lax.Precision.HIGHEST)
    return (widened + mixed).astype(jnp.bfloat16)


def local(tokens, norm_gain, gate_weight, up_weight, down_weight, expert_ids, gate_probs):
    section_index = lax.axis_index("section")
    section_count = lax.axis_size("section")
    full_tokens = lax.all_gather(tokens, "section", axis=2, tiled=True)
    micro_count, row_count, columns = full_tokens.shape
    turn_count = section_count + micro_count - 1
    norm_scale = norm_gain[0]
    w_gate = gate_weight[0]
    w_up = up_weight[0]
    w_down = down_weight[0]
    layer_ids = expert_ids[0]
    layer_probs = gate_probs[0]

    def advance(turn_index, state_pair):
        incoming, hidden_out = state_pair
        micro_index = turn_index - section_index
        is_valid = (micro_index >= 0) & (micro_index < micro_count)
        micro_pick = jnp.clip(micro_index, 0, micro_count - 1)
        fresh_rows = lax.dynamic_index_in_dim(full_tokens, micro_pick, 0, keepdims=False)
        layer_input = jnp.where(section_index == 0, fresh_rows, incoming)
        expert_list = lax.dynamic_index_in_dim(layer_ids, micro_pick, 0, keepdims=False)
        gate_share = lax.dynamic_index_in_dim(layer_probs, micro_pick, 0, keepdims=False)
        layer_output = moe_layer(
            layer_input, norm_scale, expert_list, gate_share, w_gate, w_up, w_down
        )
        updated = lax.dynamic_update_index_in_dim(hidden_out, layer_output, micro_pick, 0)
        hidden_out = jnp.where(is_valid, updated, hidden_out)
        passed = passed_along(layer_output, "section", 1)
        return (passed, hidden_out)

    initial = (
        jnp.zeros((row_count, columns), jnp.bfloat16),
        jnp.zeros((micro_count, row_count, columns), jnp.bfloat16),
    )
    final_pair = lax.fori_loop(0, turn_count, advance, initial)
    return final_pair[1][None]


def solution(mesh):
    in_specs = (
        P(None, "expert", "section"),
        P("section", None),
        P("section", "expert", None, None),
        P("section", "expert", None, None),
        P("section", "expert", None, None),
        P("section", None, "expert", None),
        P("section", None, "expert", None),
    )
    out_specs = P("section", None, "expert", None)
    return jax.shard_map(local, mesh=mesh, in_specs=in_specs, out_specs=out_specs, check_vma=False)
```

profile of v0, /device:TPU:1, one launch (start us, length us, event | category | flops | bytes accessed | tf_op | source)
XLA Modules:
  0.0 1054.6 jit_solution(3199038238281607523)
XLA Ops:
  0.0 33.3 %all_gather.3 = bf16[8,8,2048]{2,1,0:T(8,128)(2,1)} all-gather(bf16[8,8,128]{2,1,0:T(8,128)(2,1)} %param.9), channel_id=1, replica_groups=mesh['section'=16,'expert'=32] {'section'}, dimensions={2}, use_global_device_ids=true | all-gather | bytes 278528 | tf_op jit(solution)/shard_map/all_gather | solution.py:73
  34.1 1020.6 %while.17 = (s32[]{:T(128)}, bf16[8,2048]{1,0:T(8,128)(2,1)S(1)}, bf16[8,8,2048]{2,1,0:T(8,128)(2,1)}, pred[]{:T(512)}, s32[]{:T(128)}, /*index=5*/bf16[8,8,2048...) while((s32[]{:T(128)}, bf16[8,2048]{1,0:T(8,128)(2,1)S(1)}, ...), condition=%wide.region_7.8_spmd, body=%wide.region_0.7_spmd.sunk | while | flops 317443392 | bytes 22401360 | solution.py:104
  39.0 14.8 %all-to-all-start = ((bf16[32,1,2,2048]{3,2,1,0:T(2,128)(2,1)}), bf16[32,1,2,2048]{3,2,1,0:T(2,128)(2,1)S(1)}, u32[]{:S(2)}, u32[]{:S(2)}) async-start(bf16[32,1,2,2048]{3,2,1,0:T(2,128)(2,1)} %bitcast.85), calls=%async_computation | async-start | bytes 524288 | tf_op jit(solution)/shard_map/while/body/eval_jaxpr/all_to_all | solution.py:55
  72.5 8.1 all-to-all-done.1
  113.0 8.1 all-to-all-done.1
  156.2 8.1 all-to-all-done.1
  199.5 8.1 all-to-all-done.1
  242.7 8.1 all-to-all-done.1
  285.9 8.1 all-to-all-done.1
  329.1 8.1 all-to-all-done.1
  355.0 7.4 all-to-all-done
  372.3 8.1 all-to-all-done.1
  399.4 7.4 all-to-all-done
  416.7 8.1 all-to-all-done.1
  443.8 7.4 all-to-all-done
  461.1 8.1 all-to-all-done.1
  505.5 8.1 all-to-all-done.1
  532.7 7.4 all-to-all-done
  550.0 8.1 all-to-all-done.1
  594.4 8.1 all-to-all-done.1
  638.8 8.1 all-to-all-done.1
  683.2 8.1 all-to-all-done.1
  727.7 8.1 all-to-all-done.1
  772.1 8.1 all-to-all-done.1
  816.5 8.1 all-to-all-done.1
  843.6 7.4 all-to-all-done
  860.9 8.1 all-to-all-done.1
  905.4 8.1 all-to-all-done.1
  932.5 7.4 all-to-all-done
  949.8 8.1 all-to-all-done.1
  994.2 8.1 all-to-all-done.1
  1038.6 8.1 all-to-all-done.1
  (708 shorter events, 772.4 us)
Async XLA Ops:
  39.0 23.7 %all-to-all-start = ((bf16[32,1,2,2048]{3,2,1,0:T(2,128)(2,1)}), bf16[32,1,2,2048]{3,2,1,0:T(2,128)(2,1)S(1)}, u32[]{:S(2)}, u32[]{:S(2)}) async-start(bf16[32,1,2,2048]{3,2,1,0:T(2,128)(2,1)} %bitcast.85), calls=%async_computation | async-start | bytes 524288 | tf_op jit(solution)/shard_map/while/body/eval_jaxpr/all_to_all | solution.py:55
  67.9 12.8 %all-to-all-start.1 = ((bf16[1,32,2,2048]{3,2,0,1:T(2,128)(2,1)}), bf16[1,32,2,2048]{3,2,0,1:T(2,128)(2,1)S(1)}, u32[]{:S(2)}, u32[]{:S(2)}) async-start(bf16[1,32,2,2048]{3,2,0,1:T(2,128)(2,1)} %copy.31), calls=%async_computation.1 | async-start | bytes 524288 | tf_op jit(solution)/shard_map/while/body/eval_jaxpr/all_to_all | solution.py:60
  89.6 13.5 %all-to-all-start = ((bf16[32,1,2,2048]{3,2,1,0:T(2,128)(2,1)}), bf16[32,1,2,2048]{3,2,1,0:T(2,128)(2,1)S(1)}, u32[]{:S(2)}, u32[]{:S(2)}) async-start(bf16[32,1,2,2048]{3,2,1,0:T(2,128)(2,1)} %bitcast.85), calls=%async_computation | async-start | bytes 524288 | tf_op jit(solution)/shard_map/while/body/eval_jaxpr/all_to_all | solution.py:55
  108.4 12.8 %all-to-all-start.1 = ((bf16[1,32,2,2048]{3,2,0,1:T(2,128)(2,1)}), bf16[1,32,2,2048]{3,2,0,1:T(2,128)(2,1)S(1)}, u32[]{:S(2)}, u32[]{:S(2)}) async-start(bf16[1,32,2,2048]{3,2,0,1:T(2,128)(2,1)} %copy.31), calls=%async_computation.1 | async-start | bytes 524288 | tf_op jit(solution)/shard_map/while/body/eval_jaxpr/all_to_all | solution.py:60
  132.7 13.6 %all-to-all-start = ((bf16[32,1,2,2048]{3,2,1,0:T(2,128)(2,1)}), bf16[32,1,2,2048]{3,2,1,0:T(2,128)(2,1)S(1)}, u32[]{:S(2)}, u32[]{:S(2)}) async-start(bf16[32,1,2,2048]{3,2,1,0:T(2,128)(2,1)} %bitcast.85), calls=%async_computation | async-start | bytes 524288 | tf_op jit(solution)/shard_map/while/body/eval_jaxpr/all_to_all | solution.py:55
  151.6 12.8 %all-to-all-start.1 = ((bf16[1,32,2,2048]{3,2,0,1:T(2,128)(2,1)}), bf16[1,32,2,2048]{3,2,0,1:T(2,128)(2,1)S(1)}, u32[]{:S(2)}, u32[]{:S(2)}) async-start(bf16[1,32,2,2048]{3,2,0,1:T(2,128)(2,1)} %copy.31), calls=%async_computation.1 | async-start | bytes 524288 | tf_op jit(solution)/shard_map/while/body/eval_jaxpr/all_to_all | solution.py:60
  175.9 13.6 %all-to-all-start = ((bf16[32,1,2,2048]{3,2,1,0:T(2,128)(2,1)}), bf16[32,1,2,2048]{3,2,1,0:T(2,128)(2,1)S(1)}, u32[]{:S(2)}, u32[]{:S(2)}) async-start(bf16[32,1,2,2048]{3,2,1,0:T(2,128)(2,1)} %bitcast.85), calls=%async_computation | async-start | bytes 524288 | tf_op jit(solution)/shard_map/while/body/eval_jaxpr/all_to_all | solution.py:55
  194.8 12.8 %all-to-all-start.1 = ((bf16[1,32,2,2048]{3,2,0,1:T(2,128)(2,1)}), bf16[1,32,2,2048]{3,2,0,1:T(2,128)(2,1)S(1)}, u32[]{:S(2)}, u32[]{:S(2)}) async-start(bf16[1,32,2,2048]{3,2,0,1:T(2,128)(2,1)} %copy.31), calls=%async_computation.1 | async-start | bytes 524288 | tf_op jit(solution)/shard_map/while/body/eval_jaxpr/all_to_all | solution.py:60
  219.2 13.6 %all-to-all-start = ((bf16[32,1,2,2048]{3,2,1,0:T(2,128)(2,1)}), bf16[32,1,2,2048]{3,2,1,0:T(2,128)(2,1)S(1)}, u32[]{:S(2)}, u32[]{:S(2)}) async-start(bf16[32,1,2,2048]{3,2,1,0:T(2,128)(2,1)} %bitcast.85), calls=%async_computation | async-start | bytes 524288 | tf_op jit(solution)/shard_map/while/body/eval_jaxpr/all_to_all | solution.py:55
  238.0 12.8 %all-to-all-start.1 = ((bf16[1,32,2,2048]{3,2,0,1:T(2,128)(2,1)}), bf16[1,32,2,2048]{3,2,0,1:T(2,128)(2,1)S(1)}, u32[]{:S(2)}, u32[]{:S(2)}) async-start(bf16[1,32,2,2048]{3,2,0,1:T(2,128)(2,1)} %copy.31), calls=%async_computation.1 | async-start | bytes 524288 | tf_op jit(solution)/shard_map/while/body/eval_jaxpr/all_to_all | solution.py:60
  262.4 13.6 %all-to-all-start = ((bf16[32,1,2,2048]{3,2,1,0:T(2,128)(2,1)}), bf16[32,1,2,2048]{3,2,1,0:T(2,128)(2,1)S(1)}, u32[]{:S(2)}, u32[]{:S(2)}) async-start(bf16[32,1,2,2048]{3,2,1,0:T(2,128)(2,1)} %bitcast.85), calls=%async_computation | async-start | bytes 524288 | tf_op jit(solution)/shard_map/while/body/eval_jaxpr/all_to_all | solution.py:55
  305.6 13.6 %all-to-all-start = ((bf16[32,1,2,2048]{3,2,1,0:T(2,128)(2,1)}), bf16[32,1,2,2048]{3,2,1,0:T(2,128)(2,1)S(1)}, u32[]{:S(2)}, u32[]{:S(2)}) async-start(bf16[32,1,2,2048]{3,2,1,0:T(2,128)(2,1)} %bitcast.85), calls=%async_computation | async-start | bytes 524288 | tf_op jit(solution)/shard_map/while/body/eval_jaxpr/all_to_all | solution.py:55
  348.8 13.6 %all-to-all-start = ((bf16[32,1,2,2048]{3,2,1,0:T(2,128)(2,1)}), bf16[32,1,2,2048]{3,2,1,0:T(2,128)(2,1)S(1)}, u32[]{:S(2)}, u32[]{:S(2)}) async-start(bf16[32,1,2,2048]{3,2,1,0:T(2,128)(2,1)} %bitcast.85), calls=%async_computation | async-start | bytes 524288 | tf_op jit(solution)/shard_map/while/body/eval_jaxpr/all_to_all | solution.py:55
  393.2 13.6 %all-to-all-start = ((bf16[32,1,2,2048]{3,2,1,0:T(2,128)(2,1)}), bf16[32,1,2,2048]{3,2,1,0:T(2,128)(2,1)S(1)}, u32[]{:S(2)}, u32[]{:S(2)}) async-start(bf16[32,1,2,2048]{3,2,1,0:T(2,128)(2,1)} %bitcast.85), calls=%async_computation | async-start | bytes 524288 | tf_op jit(solution)/shard_map/while/body/eval_jaxpr/all_to_all | solution.py:55
  437.6 13.6 %all-to-all-start = ((bf16[32,1,2,2048]{3,2,1,0:T(2,128)(2,1)}), bf16[32,1,2,2048]{3,2,1,0:T(2,128)(2,1)S(1)}, u32[]{:S(2)}, u32[]{:S(2)}) async-start(bf16[32,1,2,2048]{3,2,1,0:T(2,128)(2,1)} %bitcast.85), calls=%async_computation | async-start | bytes 524288 | tf_op jit(solution)/shard_map/while/body/eval_jaxpr/all_to_all | solution.py:55
  482.0 13.6 %all-to-all-start = ((bf16[32,1,2,2048]{3,2,1,0:T(2,128)(2,1)}), bf16[32,1,2,2048]{3,2,1,0:T(2,128)(2,1)S(1)}, u32[]{:S(2)}, u32[]{:S(2)}) async-start(bf16[32,1,2,2048]{3,2,1,0:T(2,128)(2,1)} %bitcast.85), calls=%async_computation | async-start | bytes 524288 | tf_op jit(solution)/shard_map/while/body/eval_jaxpr/all_to_all | solution.py:55
  526.5 13.6 %all-to-all-start = ((bf16[32,1,2,2048]{3,2,1,0:T(2,128)(2,1)}), bf16[32,1,2,2048]{3,2,1,0:T(2,128)(2,1)S(1)}, u32[]{:S(2)}, u32[]{:S(2)}) async-start(bf16[32,1,2,2048]{3,2,1,0:T(2,128)(2,1)} %bitcast.85), calls=%async_computation | async-start | bytes 524288 | tf_op jit(solution)/shard_map/while/body/eval_jaxpr/all_to_all | solution.py:55
  545.3 12.8 %all-to-all-start.1 = ((bf16[1,32,2,2048]{3,2,0,1:T(2,128)(2,1)}), bf16[1,32,2,2048]{3,2,0,1:T(2,128)(2,1)S(1)}, u32[]{:S(2)}, u32[]{:S(2)}) async-start(bf16[1,32,2,2048]{3,2,0,1:T(2,128)(2,1)} %copy.31), calls=%async_computation.1 | async-start | bytes 524288 | tf_op jit(solution)/shard_map/while/body/eval_jaxpr/all_to_all | solution.py:60
  570.9 13.6 %all-to-all-start = ((bf16[32,1,2,2048]{3,2,1,0:T(2,128)(2,1)}), bf16[32,1,2,2048]{3,2,1,0:T(2,128)(2,1)S(1)}, u32[]{:S(2)}, u32[]{:S(2)}) async-start(bf16[32,1,2,2048]{3,2,1,0:T(2,128)(2,1)} %bitcast.85), calls=%async_computation | async-start | bytes 524288 | tf_op jit(solution)/shard_map/while/body/eval_jaxpr/all_to_all | solution.py:55
  615.3 13.6 %all-to-all-start = ((bf16[32,1,2,2048]{3,2,1,0:T(2,128)(2,1)}), bf16[32,1,2,2048]{3,2,1,0:T(2,128)(2,1)S(1)}, u32[]{:S(2)}, u32[]{:S(2)}) async-start(bf16[32,1,2,2048]{3,2,1,0:T(2,128)(2,1)} %bitcast.85), calls=%async_computation | async-start | bytes 524288 | tf_op jit(solution)/shard_map/while/body/eval_jaxpr/all_to_all | solution.py:55
  659.7 13.6 %all-to-all-start = ((bf16[32,1,2,2048]{3,2,1,0:T(2,128)(2,1)}), bf16[32,1,2,2048]{3,2,1,0:T(2,128)(2,1)S(1)}, u32[]{:S(2)}, u32[]{:S(2)}) async-start(bf16[32,1,2,2048]{3,2,1,0:T(2,128)(2,1)} %bitcast.85), calls=%async_computation | async-start | bytes 524288 | tf_op jit(solution)/shard_map/while/body/eval_jaxpr/all_to_all | solution.py:55
  704.2 13.6 %all-to-all-start = ((bf16[32,1,2,2048]{3,2,1,0:T(2,128)(2,1)}), bf16[32,1,2,2048]{3,2,1,0:T(2,128)(2,1)S(1)}, u32[]{:S(2)}, u32[]{:S(2)}) async-start(bf16[32,1,2,2048]{3,2,1,0:T(2,128)(2,1)} %bitcast.85), calls=%async_computation | async-start | bytes 524288 | tf_op jit(solution)/shard_map/while/body/eval_jaxpr/all_to_all | solution.py:55
  723.0 12.8 %all-to-all-start.1 = ((bf16[1,32,2,2048]{3,2,0,1:T(2,128)(2,1)}), bf16[1,32,2,2048]{3,2,0,1:T(2,128)(2,1)S(1)}, u32[]{:S(2)}, u32[]{:S(2)}) async-start(bf16[1,32,2,2048]{3,2,0,1:T(2,128)(2,1)} %copy.31), calls=%async_computation.1 | async-start | bytes 524288 | tf_op jit(solution)/shard_map/while/body/eval_jaxpr/all_to_all | solution.py:60
  748.6 13.6 %all-to-all-start = ((bf16[32,1,2,2048]{3,2,1,0:T(2,128)(2,1)}), bf16[32,1,2,2048]{3,2,1,0:T(2,128)(2,1)S(1)}, u32[]{:S(2)}, u32[]{:S(2)}) async-start(bf16[32,1,2,2048]{3,2,1,0:T(2,128)(2,1)} %bitcast.85), calls=%async_computation | async-start | bytes 524288 | tf_op jit(solution)/shard_map/while/body/eval_jaxpr/all_to_all | solution.py:55
  793.0 13.6 %all-to-all-start = ((bf16[32,1,2,2048]{3,2,1,0:T(2,128)(2,1)}), bf16[32,1,2,2048]{3,2,1,0:T(2,128)(2,1)S(1)}, u32[]{:S(2)}, u32[]{:S(2)}) async-start(bf16[32,1,2,2048]{3,2,1,0:T(2,128)(2,1)} %bitcast.85), calls=%async_computation | async-start | bytes 524288 | tf_op jit(solution)/shard_map/while/body/eval_jaxpr/all_to_all | solution.py:55
  811.9 12.8 %all-to-all-start.1 = ((bf16[1,32,2,2048]{3,2,0,1:T(2,128)(2,1)}), bf16[1,32,2,2048]{3,2,0,1:T(2,128)(2,1)S(1)}, u32[]{:S(2)}, u32[]{:S(2)}) async-start(bf16[1,32,2,2048]{3,2,0,1:T(2,128)(2,1)} %copy.31), calls=%async_computation.1 | async-start | bytes 524288 | tf_op jit(solution)/shard_map/while/body/eval_jaxpr/all_to_all | solution.py:60
  837.4 13.6 %all-to-all-start = ((bf16[32,1,2,2048]{3,2,1,0:T(2,128)(2,1)}), bf16[32,1,2,2048]{3,2,1,0:T(2,128)(2,1)S(1)}, u32[]{:S(2)}, u32[]{:S(2)}) async-start(bf16[32,1,2,2048]{3,2,1,0:T(2,128)(2,1)} %bitcast.85), calls=%async_computation | async-start | bytes 524288 | tf_op jit(solution)/shard_map/while/body/eval_jaxpr/all_to_all | solution.py:55
  881.9 13.6 %all-to-all-start = ((bf16[32,1,2,2048]{3,2,1,0:T(2,128)(2,1)}), bf16[32,1,2,2048]{3,2,1,0:T(2,128)(2,1)S(1)}, u32[]{:S(2)}, u32[]{:S(2)}) async-start(bf16[32,1,2,2048]{3,2,1,0:T(2,128)(2,1)} %bitcast.85), calls=%async_computation | async-start | bytes 524288 | tf_op jit(solution)/shard_map/while/body/eval_jaxpr/all_to_all | solution.py:55
  900.7 12.8 %all-to-all-start.1 = ((bf16[1,32,2,2048]{3,2,0,1:T(2,128)(2,1)}), bf16[1,32,2,2048]{3,2,0,1:T(2,128)(2,1)S(1)}, u32[]{:S(2)}, u32[]{:S(2)}) async-start(bf16[1,32,2,2048]{3,2,0,1:T(2,128)(2,1)} %copy.31), calls=%async_computation.1 | async-start | bytes 524288 | tf_op jit(solution)/shard_map/while/body/eval_jaxpr/all_to_all | solution.py:60
  926.3 13.6 %all-to-all-start = ((bf16[32,1,2,2048]{3,2,1,0:T(2,128)(2,1)}), bf16[32,1,2,2048]{3,2,1,0:T(2,128)(2,1)S(1)}, u32[]{:S(2)}, u32[]{:S(2)}) async-start(bf16[32,1,2,2048]{3,2,1,0:T(2,128)(2,1)} %bitcast.85), calls=%async_computation | async-start | bytes 524288 | tf_op jit(solution)/shard_map/while/body/eval_jaxpr/all_to_all | solution.py:55
  970.7 13.6 %all-to-all-start = ((bf16[32,1,2,2048]{3,2,1,0:T(2,128)(2,1)}), bf16[32,1,2,2048]{3,2,1,0:T(2,128)(2,1)S(1)}, u32[]{:S(2)}, u32[]{:S(2)}) async-start(bf16[32,1,2,2048]{3,2,1,0:T(2,128)(2,1)} %bitcast.85), calls=%async_computation | async-start | bytes 524288 | tf_op jit(solution)/shard_map/while/body/eval_jaxpr/all_to_all | solution.py:55
  1015.1 13.6 %all-to-all-start = ((bf16[32,1,2,2048]{3,2,1,0:T(2,128)(2,1)}), bf16[32,1,2,2048]{3,2,1,0:T(2,128)(2,1)S(1)}, u32[]{:S(2)}, u32[]{:S(2)}) async-start(bf16[32,1,2,2048]{3,2,1,0:T(2,128)(2,1)} %bitcast.85), calls=%async_computation | async-start | bytes 524288 | tf_op jit(solution)/shard_map/while/body/eval_jaxpr/all_to_all | solution.py:55
  (83 other events, 1104.7 us)
where the time goes:
time: 1070 us; the launch traced here: 1050 us
  waiting for transfers between devices  381 us (36%)
  starting transfers between devices  310 us (29%)
  matrix products  138 us (13%)
  other arithmetic  102 us (10%)
  local copies, waits for them, and re-layouts  89 us (8%)
  blocking collectives  33.3 us (3%)
    all_to_all x23, waiting for transfers between devices, moe_layer(): lax.all_to_all(results, 'expert', split_axis=1, concat_axis=0, tiled=True)  187 us
    all_to_all x23, waiting for transfers between devices, moe_layer(): lax.all_to_all(sending, 'expert', split_axis=0, concat_axis=1, tiled=True)  171 us
    all_to_all x23, starting transfers between devices, moe_layer(): lax.all_to_all(sending, 'expert', split_axis=0, concat_axis=1, tiled=True)  116 us
    ppermute x23, starting transfers between devices, passed_along(): return lax.ppermute(value, axis, pairs)  107 us
    all_to_all x23, starting transfers between devices, moe_layer(): lax.all_to_all(results, 'expert', split_axis=1, concat_axis=0, tiled=True)  86.4 us
    convert_element_type x23, local copies, waits for them, and re-layouts, expert_block(): jnp.einsum('escf,efd->escd', active, w_down, preferred_element_type=jnp.f...  44.2 us
    dot_general x23, matrix products, expert_block(): jnp.einsum('escd,edf->escf', routed, w_gate, preferred_element_type=jnp.f...  40.6 us
    dot_general x23, matrix products, moe_layer(): mixed = jnp.dot(mixing, returns_wide, precision=lax.Precision.HIGHEST)  36.9 us
  transfers between devices with their start and end apart: 69, of which 69 were waited for; matrix products, arithmetic and copies ran while one was open for 5% of the time, Pallas kernels for 0%

commit v1 on v0

--- a/solution.py
+++ b/solution.py
@@ -24,15 +24,15 @@
     )
 
 
-def slot_numbers(flat_ids, experts, capacity):
-    onehot = (flat_ids[..., None] == jnp.arange(experts, dtype=jnp.int32)).astype(jnp.int32)
-    before = jnp.cumsum(onehot, axis=-2) - onehot
-    return flat_ids * capacity + jnp.sum(onehot * before, axis=-1)
+def slot_numbers(expert_list, capacity):
+    same = (expert_list[:, None, :, None] == expert_list[None, :, None, :]).any(axis=3)
+    rows = jnp.arange(expert_list.shape[0])
+    earlier = same & (rows[None, :] < rows[:, None])[:, :, None]
+    return expert_list * capacity + jnp.sum(earlier.astype(jnp.int32), axis=1)
 
 
 def moe_layer(layer_input, norm_scale, expert_list, gate_share, w_gate, w_up, w_down):
     row_count, columns = layer_input.shape
-    top_count = expert_list.shape[1]
     experts_local = w_gate.shape[0]
     groups = lax.axis_size("expert")
     experts = experts_local * groups
@@ -42,9 +42,7 @@
         widened * lax.rsqrt(jnp.mean(widened * widened, axis=-1, keepdims=True) + EPS) * norm_scale
     ).astype(jnp.bfloat16)
     weight = gate_share / jnp.sum(gate_share, axis=-1, keepdims=True)
-    slot_index = slot_numbers(
-        expert_list.reshape(row_count * top_count), experts, capacity
-    ).reshape(row_count, top_count)
+    slot_index = slot_numbers(expert_list, capacity)
     target = jnp.arange(experts * capacity, dtype=jnp.int32)
     placement = jnp.sum(
         (slot_index[None, :, :] == target[:, None, None]).astype(jnp.bfloat16), axis=2

time: 1070 us -> 1090 us (1.019)
  other arithmetic: 102 us -> 124 us
    reduce_or x0 -> x23, other arithmetic: none -> 28.5 us  [slot_numbers(): (expert_list[:, None, :, None] == expert_list[None, :, None, :]).any(axis=3)]
    dynamic_slice x23 -> x0, local copies, waits for them, and re-layouts: 15.8 us -> none  [advance(): lax.dynamic_index_in_dim(layer_ids, micro_pick, 0, keepdims=False)]
    squeeze x0 -> x23, local copies, waits for them, and re-layouts: none -> 15.8 us  [advance(): lax.dynamic_index_in_dim(layer_ids, micro_pick, 0, keepdims=False)]
where the time goes in v1:
time: 1090 us; the launch traced here: 1070 us
  waiting for transfers between devices  383 us (35%)
  starting transfers between devices  310 us (28%)
  matrix products  138 us (13%)
  other arithmetic  124 us (11%)
  local copies, waits for them, and re-layouts  83.5 us (8%)
  blocking collectives  33.3 us (3%)
    all_to_all x23, waiting for transfers between devices, moe_layer(): lax.all_to_all(results, 'expert', split_axis=1, concat_axis=0, tiled=True)  187 us
    all_to_all x23, waiting for transfers between devices, moe_layer(): lax.all_to_all(sending, 'expert', split_axis=0, concat_axis=1, tiled=True)  172 us
    all_to_all x23, starting transfers between devices, moe_layer(): lax.all_to_all(sending, 'expert', split_axis=0, concat_axis=1, tiled=True)  116 us
    ppermute x23, starting transfers between devices, passed_along(): return lax.ppermute(value, axis, pairs)  107 us
    all_to_all x23, starting transfers between devices, moe_layer(): lax.all_to_all(results, 'expert', split_axis=1, concat_axis=0, tiled=True)  86.5 us
    convert_element_type x23, local copies, waits for them, and re-layouts, expert_block(): jnp.einsum('escf,efd->escd', active, w_down, preferred_element_type=jnp.f...  44.2 us
    dot_general x23, matrix products, expert_block(): jnp.einsum('escd,edf->escf', routed, w_gate, preferred_element_type=jnp.f...  40.6 us
    dot_general x23, matrix products, moe_layer(): mixed = jnp.dot(mixing, returns_wide, precision=lax.Precision.HIGHEST)  36.9 us
  transfers between devices with their start and end apart: 69, of which 69 were waited for; matrix products, arithmetic and copies ran while one was open for 5% of the time, Pallas kernels for 0%

profile of v1, /device:TPU:1, one launch (start us, length us, event | category | flops | bytes accessed | tf_op | source)
XLA Modules:
  0.0 1073.4 jit_solution(4948942139263468010)
XLA Ops:
  0.0 33.3 %all_gather.3 = bf16[8,8,2048]{2,1,0:T(8,128)(2,1)} all-gather(bf16[8,8,128]{2,1,0:T(8,128)(2,1)} %param.9), channel_id=1, replica_groups=mesh['section'=16,'expert'=32] {'section'}, dimensions={2}, use_global_device_ids=true | all-gather | bytes 278528 | tf_op jit(solution)/shard_map/all_gather | solution.py:71
  34.1 1039.4 %while.17 = (s32[]{:T(128)}, bf16[8,2048]{1,0:T(8,128)(2,1)S(1)}, bf16[8,8,2048]{2,1,0:T(8,128)(2,1)}, pred[]{:T(512)}, s32[]{:T(128)}, /*index=5*/bf16[8,8,2048...) while((s32[]{:T(128)}, bf16[8,2048]{1,0:T(8,128)(2,1)S(1)}, ...), condition=%wide.region_7.8_spmd, body=%wide.region_0.7_spmd.sunk | while | flops 317309312 | bytes 22367948 | solution.py:102
  39.8 14.8 %all-to-all-start = ((bf16[32,1,2,2048]{3,2,1,0:T(2,128)(2,1)}), bf16[32,1,2,2048]{3,2,1,0:T(2,128)(2,1)S(1)}, u32[]{:S(2)}, u32[]{:S(2)}) async-start(bf16[32,1,2,2048]{3,2,1,0:T(2,128)(2,1)} %bitcast.95), calls=%async_computation | async-start | bytes 524288 | tf_op jit(solution)/shard_map/while/body/eval_jaxpr/all_to_all | solution.py:53
  73.4 8.1 all-to-all-done.1
  114.7 8.1 all-to-all-done.1
  158.7 8.1 all-to-all-done.1
  202.7 8.1 all-to-all-done.1
  229.4 7.5 all-to-all-done
  246.8 8.1 all-to-all-done.1
  273.4 7.5 all-to-all-done
  290.8 8.1 all-to-all-done.1
  317.4 7.5 all-to-all-done
  334.8 8.1 all-to-all-done.1
  378.9 8.1 all-to-all-done.1
  424.0 8.1 all-to-all-done.1
  451.9 7.5 all-to-all-done
  469.3 8.1 all-to-all-done.1
  514.5 8.1 all-to-all-done.1
  559.8 8.1 all-to-all-done.1
  605.0 8.1 all-to-all-done.1
  632.9 7.5 all-to-all-done
  650.2 8.1 all-to-all-done.1
  695.5 8.1 all-to-all-done.1
  740.7 8.1 all-to-all-done.1
  786.0 8.1 all-to-all-done.1
  813.8 7.5 all-to-all-done
  831.2 8.1 all-to-all-done.1
  876.5 8.1 all-to-all-done.1
  921.7 8.1 all-to-all-done.1
  966.9 8.1 all-to-all-done.1
  1012.2 8.1 all-to-all-done.1
  1057.4 8.1 all-to-all-done.1
  (639 shorter events, 790.6 us)
Async XLA Ops:
  39.8 23.7 %all-to-all-start = ((bf16[32,1,2,2048]{3,2,1,0:T(2,128)(2,1)}), bf16[32,1,2,2048]{3,2,1,0:T(2,128)(2,1)S(1)}, u32[]{:S(2)}, u32[]{:S(2)}) async-start(bf16[32,1,2,2048]{3,2,1,0:T(2,128)(2,1)} %bitcast.95), calls=%async_computation | async-start | bytes 524288 | tf_op jit(solution)/shard_map/while/body/eval_jaxpr/all_to_all | solution.py:53
  91.2 13.5 %all-to-all-start = ((bf16[32,1,2,2048]{3,2,1,0:T(2,128)(2,1)}), bf16[32,1,2,2048]{3,2,1,0:T(2,128)(2,1)S(1)}, u32[]{:S(2)}, u32[]{:S(2)}) async-start(bf16[32,1,2,2048]{3,2,1,0:T(2,128)(2,1)} %bitcast.95), calls=%async_computation | async-start | bytes 524288 | tf_op jit(solution)/shard_map/while/body/eval_jaxpr/all_to_all | solution.py:53
  110.0 12.8 %all-to-all-start.1 = ((bf16[1,32,2,2048]{3,2,0,1:T(2,128)(2,1)}), bf16[1,32,2,2048]{3,2,0,1:T(2,128)(2,1)S(1)}, u32[]{:S(2)}, u32[]{:S(2)}) async-start(bf16[1,32,2,2048]{3,2,0,1:T(2,128)(2,1)} %copy.31), calls=%async_computation.1 | async-start | bytes 524288 | tf_op jit(solution)/shard_map/while/body/eval_jaxpr/all_to_all | solution.py:58
  135.2 13.6 %all-to-all-start = ((bf16[32,1,2,2048]{3,2,1,0:T(2,128)(2,1)}), bf16[32,1,2,2048]{3,2,1,0:T(2,128)(2,1)S(1)}, u32[]{:S(2)}, u32[]{:S(2)}) async-start(bf16[32,1,2,2048]{3,2,1,0:T(2,128)(2,1)} %bitcast.95), calls=%async_computation | async-start | bytes 524288 | tf_op jit(solution)/shard_map/while/body/eval_jaxpr/all_to_all | solution.py:53
  179.2 13.6 %all-to-all-start = ((bf16[32,1,2,2048]{3,2,1,0:T(2,128)(2,1)}), bf16[32,1,2,2048]{3,2,1,0:T(2,128)(2,1)S(1)}, u32[]{:S(2)}, u32[]{:S(2)}) async-start(bf16[32,1,2,2048]{3,2,1,0:T(2,128)(2,1)} %bitcast.95), calls=%async_computation | async-start | bytes 524288 | tf_op jit(solution)/shard_map/while/body/eval_jaxpr/all_to_all | solution.py:53
  198.1 12.8 %all-to-all-start.1 = ((bf16[1,32,2,2048]{3,2,0,1:T(2,128)(2,1)}), bf16[1,32,2,2048]{3,2,0,1:T(2,128)(2,1)S(1)}, u32[]{:S(2)}, u32[]{:S(2)}) async-start(bf16[1,32,2,2048]{3,2,0,1:T(2,128)(2,1)} %copy.31), calls=%async_computation.1 | async-start | bytes 524288 | tf_op jit(solution)/shard_map/while/body/eval_jaxpr/all_to_all | solution.py:58
  223.2 13.6 %all-to-all-start = ((bf16[32,1,2,2048]{3,2,1,0:T(2,128)(2,1)}), bf16[32,1,2,2048]{3,2,1,0:T(2,128)(2,1)S(1)}, u32[]{:S(2)}, u32[]{:S(2)}) async-start(bf16[32,1,2,2048]{3,2,1,0:T(2,128)(2,1)} %bitcast.95), calls=%async_computation | async-start | bytes 524288 | tf_op jit(solution)/shard_map/while/body/eval_jaxpr/all_to_all | solution.py:53
  242.1 12.8 %all-to-all-start.1 = ((bf16[1,32,2,2048]{3,2,0,1:T(2,128)(2,1)}), bf16[1,32,2,2048]{3,2,0,1:T(2,128)(2,1)S(1)}, u32[]{:S(2)}, u32[]{:S(2)}) async-start(bf16[1,32,2,2048]{3,2,0,1:T(2,128)(2,1)} %copy.31), calls=%async_computation.1 | async-start | bytes 524288 | tf_op jit(solution)/shard_map/while/body/eval_jaxpr/all_to_all | solution.py:58
  267.3 13.6 %all-to-all-start = ((bf16[32,1,2,2048]{3,2,1,0:T(2,128)(2,1)}), bf16[32,1,2,2048]{3,2,1,0:T(2,128)(2,1)S(1)}, u32[]{:S(2)}, u32[]{:S(2)}) async-start(bf16[32,1,2,2048]{3,2,1,0:T(2,128)(2,1)} %bitcast.95), calls=%async_computation | async-start | bytes 524288 | tf_op jit(solution)/shard_map/while/body/eval_jaxpr/all_to_all | solution.py:53
  286.2 12.8 %all-to-all-start.1 = ((bf16[1,32,2,2048]{3,2,0,1:T(2,128)(2,1)}), bf16[1,32,2,2048]{3,2,0,1:T(2,128)(2,1)S(1)}, u32[]{:S(2)}, u32[]{:S(2)}) async-start(bf16[1,32,2,2048]{3,2,0,1:T(2,128)(2,1)} %copy.31), calls=%async_computation.1 | async-start | bytes 524288 | tf_op jit(solution)/shard_map/while/body/eval_jaxpr/all_to_all | solution.py:58
  311.3 13.6 %all-to-all-start = ((bf16[32,1,2,2048]{3,2,1,0:T(2,128)(2,1)}), bf16[32,1,2,2048]{3,2,1,0:T(2,128)(2,1)S(1)}, u32[]{:S(2)}, u32[]{:S(2)}) async-start(bf16[32,1,2,2048]{3,2,1,0:T(2,128)(2,1)} %bitcast.95), calls=%async_computation | async-start | bytes 524288 | tf_op jit(solution)/shard_map/while/body/eval_jaxpr/all_to_all | solution.py:53
  330.2 12.8 %all-to-all-start.1 = ((bf16[1,32,2,2048]{3,2,0,1:T(2,128)(2,1)}), bf16[1,32,2,2048]{3,2,0,1:T(2,128)(2,1)S(1)}, u32[]{:S(2)}, u32[]{:S(2)}) async-start(bf16[1,32,2,2048]{3,2,0,1:T(2,128)(2,1)} %copy.31), calls=%async_computation.1 | async-start | bytes 524288 | tf_op jit(solution)/shard_map/while/body/eval_jaxpr/all_to_all | solution.py:58
  355.3 13.6 %all-to-all-start = ((bf16[32,1,2,2048]{3,2,1,0:T(2,128)(2,1)}), bf16[32,1,2,2048]{3,2,1,0:T(2,128)(2,1)S(1)}, u32[]{:S(2)}, u32[]{:S(2)}) async-start(bf16[32,1,2,2048]{3,2,1,0:T(2,128)(2,1)} %bitcast.95), calls=%async_computation | async-start | bytes 524288 | tf_op jit(solution)/shard_map/while/body/eval_jaxpr/all_to_all | solution.py:53
  374.2 12.8 %all-to-all-start.1 = ((bf16[1,32,2,2048]{3,2,0,1:T(2,128)(2,1)}), bf16[1,32,2,2048]{3,2,0,1:T(2,128)(2,1)S(1)}, u32[]{:S(2)}, u32[]{:S(2)}) async-start(bf16[1,32,2,2048]{3,2,0,1:T(2,128)(2,1)} %copy.31), calls=%async_computation.1 | async-start | bytes 524288 | tf_op jit(solution)/shard_map/while/body/eval_jaxpr/all_to_all | solution.py:58
  400.5 13.6 %all-to-all-start = ((bf16[32,1,2,2048]{3,2,1,0:T(2,128)(2,1)}), bf16[32,1,2,2048]{3,2,1,0:T(2,128)(2,1)S(1)}, u32[]{:S(2)}, u32[]{:S(2)}) async-start(bf16[32,1,2,2048]{3,2,1,0:T(2,128)(2,1)} %bitcast.95), calls=%async_computation | async-start | bytes 524288 | tf_op jit(solution)/shard_map/while/body/eval_jaxpr/all_to_all | solution.py:53
  419.4 12.8 %all-to-all-start.1 = ((bf16[1,32,2,2048]{3,2,0,1:T(2,128)(2,1)}), bf16[1,32,2,2048]{3,2,0,1:T(2,128)(2,1)S(1)}, u32[]{:S(2)}, u32[]{:S(2)}) async-start(bf16[1,32,2,2048]{3,2,0,1:T(2,128)(2,1)} %copy.31), calls=%async_computation.1 | async-start | bytes 524288 | tf_op jit(solution)/shard_map/while/body/eval_jaxpr/all_to_all | solution.py:58
  445.8 13.6 %all-to-all-start = ((bf16[32,1,2,2048]{3,2,1,0:T(2,128)(2,1)}), bf16[32,1,2,2048]{3,2,1,0:T(2,128)(2,1)S(1)}, u32[]{:S(2)}, u32[]{:S(2)}) async-start(bf16[32,1,2,2048]{3,2,1,0:T(2,128)(2,1)} %bitcast.95), calls=%async_computation | async-start | bytes 524288 | tf_op jit(solution)/shard_map/while/body/eval_jaxpr/all_to_all | solution.py:53
  491.0 13.6 %all-to-all-start = ((bf16[32,1,2,2048]{3,2,1,0:T(2,128)(2,1)}), bf16[32,1,2,2048]{3,2,1,0:T(2,128)(2,1)S(1)}, u32[]{:S(2)}, u32[]{:S(2)}) async-start(bf16[32,1,2,2048]{3,2,1,0:T(2,128)(2,1)} %bitcast.95), calls=%async_computation | async-start | bytes 524288 | tf_op jit(solution)/shard_map/while/body/eval_jaxpr/all_to_all | solution.py:53
  536.2 13.6 %all-to-all-start = ((bf16[32,1,2,2048]{3,2,1,0:T(2,128)(2,1)}), bf16[32,1,2,2048]{3,2,1,0:T(2,128)(2,1)S(1)}, u32[]{:S(2)}, u32[]{:S(2)}) async-start(bf16[32,1,2,2048]{3,2,1,0:T(2,128)(2,1)} %bitcast.95), calls=%async_computation | async-start | bytes 524288 | tf_op jit(solution)/shard_map/while/body/eval_jaxpr/all_to_all | solution.py:53
  581.5 13.6 %all-to-all-start = ((bf16[32,1,2,2048]{3,2,1,0:T(2,128)(2,1)}), bf16[32,1,2,2048]{3,2,1,0:T(2,128)(2,1)S(1)}, u32[]{:S(2)}, u32[]{:S(2)}) async-start(bf16[32,1,2,2048]{3,2,1,0:T(2,128)(2,1)} %bitcast.95), calls=%async_computation | async-start | bytes 524288 | tf_op jit(solution)/shard_map/while/body/eval_jaxpr/all_to_all | solution.py:53
  626.7 13.6 %all-to-all-start = ((bf16[32,1,2,2048]{3,2,1,0:T(2,128)(2,1)}), bf16[32,1,2,2048]{3,2,1,0:T(2,128)(2,1)S(1)}, u32[]{:S(2)}, u32[]{:S(2)}) async-start(bf16[32,1,2,2048]{3,2,1,0:T(2,128)(2,1)} %bitcast.95), calls=%async_computation | async-start | bytes 524288 | tf_op jit(solution)/shard_map/while/body/eval_jaxpr/all_to_all | solution.py:53
  672.0 13.6 %all-to-all-start = ((bf16[32,1,2,2048]{3,2,1,0:T(2,128)(2,1)}), bf16[32,1,2,2048]{3,2,1,0:T(2,128)(2,1)S(1)}, u32[]{:S(2)}, u32[]{:S(2)}) async-start(bf16[32,1,2,2048]{3,2,1,0:T(2,128)(2,1)} %bitcast.95), calls=%async_computation | async-start | bytes 524288 | tf_op jit(solution)/shard_map/while/body/eval_jaxpr/all_to_all | solution.py:53
  717.2 13.6 %all-to-all-start = ((bf16[32,1,2,2048]{3,2,1,0:T(2,128)(2,1)}), bf16[32,1,2,2048]{3,2,1,0:T(2,128)(2,1)S(1)}, u32[]{:S(2)}, u32[]{:S(2)}) async-start(bf16[32,1,2,2048]{3,2,1,0:T(2,128)(2,1)} %bitcast.95), calls=%async_computation | async-start | bytes 524288 | tf_op jit(solution)/shard_map/while/body/eval_jaxpr/all_to_all | solution.py:53
  762.5 13.6 %all-to-all-start = ((bf16[32,1,2,2048]{3,2,1,0:T(2,128)(2,1)}), bf16[32,1,2,2048]{3,2,1,0:T(2,128)(2,1)S(1)}, u32[]{:S(2)}, u32[]{:S(2)}) async-start(bf16[32,1,2,2048]{3,2,1,0:T(2,128)(2,1)} %bitcast.95), calls=%async_computation | async-start | bytes 524288 | tf_op jit(solution)/shard_map/while/body/eval_jaxpr/all_to_all | solution.py:53
  781.3 12.8 %all-to-all-start.1 = ((bf16[1,32,2,2048]{3,2,0,1:T(2,128)(2,1)}), bf16[1,32,2,2048]{3,2,0,1:T(2,128)(2,1)S(1)}, u32[]{:S(2)}, u32[]{:S(2)}) async-start(bf16[1,32,2,2048]{3,2,0,1:T(2,128)(2,1)} %copy.31), calls=%async_computation.1 | async-start | bytes 524288 | tf_op jit(solution)/shard_map/while/body/eval_jaxpr/all_to_all | solution.py:58
  807.7 13.6 %all-to-all-start = ((bf16[32,1,2,2048]{3,2,1,0:T(2,128)(2,1)}), bf16[32,1,2,2048]{3,2,1,0:T(2,128)(2,1)S(1)}, u32[]{:S(2)}, u32[]{:S(2)}) async-start(bf16[32,1,2,2048]{3,2,1,0:T(2,128)(2,1)} %bitcast.95), calls=%async_computation | async-start | bytes 524288 | tf_op jit(solution)/shard_map/while/body/eval_jaxpr/all_to_all | solution.py:53
  853.0 13.6 %all-to-all-start = ((bf16[32,1,2,2048]{3,2,1,0:T(2,128)(2,1)}), bf16[32,1,2,2048]{3,2,1,0:T(2,128)(2,1)S(1)}, u32[]{:S(2)}, u32[]{:S(2)}) async-start(bf16[32,1,2,2048]{3,2,1,0:T(2,128)(2,1)} %bitcast.95), calls=%async_computation | async-start | bytes 524288 | tf_op jit(solution)/shard_map/while/body/eval_jaxpr/all_to_all | solution.py:53
  898.2 13.6 %all-to-all-start = ((bf16[32,1,2,2048]{3,2,1,0:T(2,128)(2,1)}), bf16[32,1,2,2048]{3,2,1,0:T(2,128)(2,1)S(1)}, u32[]{:S(2)}, u32[]{:S(2)}) async-start(bf16[32,1,2,2048]{3,2,1,0:T(2,128)(2,1)} %bitcast.95), calls=%async_computation | async-start | bytes 524288 | tf_op jit(solution)/shard_map/while/body/eval_jaxpr/all_to_all | solution.py:53
  943.4 13.6 %all-to-all-start = ((bf16[32,1,2,2048]{3,2,1,0:T(2,128)(2,1)}), bf16[32,1,2,2048]{3,2,1,0:T(2,128)(2,1)S(1)}, u32[]{:S(2)}, u32[]{:S(2)}) async-start(bf16[32,1,2,2048]{3,2,1,0:T(2,128)(2,1)} %bitcast.95), calls=%async_computation | async-start | bytes 524288 | tf_op jit(solution)/shard_map/while/body/eval_jaxpr/all_to_all | solution.py:53
  962.3 12.8 %all-to-all-start.1 = ((bf16[1,32,2,2048]{3,2,0,1:T(2,128)(2,1)}), bf16[1,32,2,2048]{3,2,0,1:T(2,128)(2,1)S(1)}, u32[]{:S(2)}, u32[]{:S(2)}) async-start(bf16[1,32,2,2048]{3,2,0,1:T(2,128)(2,1)} %copy.31), calls=%async_computation.1 | async-start | bytes 524288 | tf_op jit(solution)/shard_map/while/body/eval_jaxpr/all_to_all | solution.py:58
  988.7 13.6 %all-to-all-start = ((bf16[32,1,2,2048]{3,2,1,0:T(2,128)(2,1)}), bf16[32,1,2,2048]{3,2,1,0:T(2,128)(2,1)S(1)}, u32[]{:S(2)}, u32[]{:S(2)}) async-start(bf16[32,1,2,2048]{3,2,1,0:T(2,128)(2,1)} %bitcast.95), calls=%async_computation | async-start | bytes 524288 | tf_op jit(solution)/shard_map/while/body/eval_jaxpr/all_to_all | solution.py:53
  1033.9 13.6 %all-to-all-start = ((bf16[32,1,2,2048]{3,2,1,0:T(2,128)(2,1)}), bf16[32,1,2,2048]{3,2,1,0:T(2,128)(2,1)S(1)}, u32[]{:S(2)}, u32[]{:S(2)}) async-start(bf16[32,1,2,2048]{3,2,1,0:T(2,128)(2,1)} %bitcast.95), calls=%async_computation | async-start | bytes 524288 | tf_op jit(solution)/shard_map/while/body/eval_jaxpr/all_to_all | solution.py:53
  (83 other events, 1104.6 us)

commit v2 on v1

v2 whole, which is shorter than its diff:
```python
import jax
import jax.numpy as jnp
from jax import lax
from jax.experimental import pallas as pl
from jax.experimental.pallas import tpu as pltpu
from jax.sharding import PartitionSpec as P

CAP = 2
EPS = 1e-06
LANES = 128
GROUP = 2

VMEM = pl.BlockSpec(memory_space=pltpu.VMEM)
SMEM = pl.BlockSpec(memory_space=pltpu.SMEM)


def place_kernel(turn_ref, row_ref, x_ref, gain_ref, send_ref, normed_ref):
    experts, slots, parts, lanes = send_ref.shape
    wide = x_ref[...].astype(jnp.float32)
    mean = jnp.sum(wide * wide, axis=(1, 2), keepdims=True) * (1.0 / (parts * lanes))
    normed = wide * lax.rsqrt(mean + EPS) * gain_ref[...][None]
    normed_ref[...] = normed.astype(jnp.bfloat16)
    pick = turn_ref[0]
    for e in range(experts):
        for q in range(slots):
            send_ref[e, q] = normed_ref[row_ref[pick, e * slots + q]]


def expert_kernel(recv_ref, gate_ref, up_ref, down_ref, out_ref, wide_ref):
    rows, parts, lanes = recv_ref.shape
    wide_ref[...] = recv_ref[...].astype(jnp.float32).reshape(rows * parts, lanes)
    routed = jnp.concatenate(
        [wide_ref[pl.ds(c, rows, stride=parts), :].astype(jnp.bfloat16) for c in range(parts)],
        axis=1,
    )
    gate = jnp.dot(routed, gate_ref[...], preferred_element_type=jnp.float32)
    up = jnp.dot(routed, up_ref[...], preferred_element_type=jnp.float32)
    active = (gate / (1.0 + jnp.exp(-gate)) * up).astype(jnp.bfloat16)
    result = jnp.dot(active, down_ref[...], preferred_element_type=jnp.float32)
    for c in range(parts):
        wide_ref[pl.ds(c, rows, stride=parts), :] = result[:, c * lanes : (c + 1) * lanes]
    out_ref[...] = wide_ref[...].reshape(rows, parts, lanes).astype(jnp.bfloat16)


def mix_kernel(turn_ref, slot_ref, share_ref, ret_ref, x_ref, out_ref):
    rows = x_ref.shape[0]
    top = slot_ref.shape[1] // rows
    pick = turn_ref[0]
    for r in range(rows):
        total = x_ref[r].astype(jnp.float32)
        for k in range(top):
            part = ret_ref[slot_ref[pick, r * top + k]].astype(jnp.float32)
            total = total + share_ref[pick, r * top + k] * part
        out_ref[r] = total.astype(jnp.bfloat16)


def tables(expert_list, gate_probs, experts):
    micro, rows, _ = expert_list.shape
    groups = micro // GROUP
    number = jnp.arange(rows)
    member = (jnp.arange(micro) % GROUP)[:, None, None]
    chosen = expert_list[..., None] == jnp.arange(experts)
    named = chosen.any(axis=2)
    first = jnp.min(jnp.where(named, number[None, :, None], rows - 1), axis=1)
    last = jnp.max(jnp.where(named, number[None, :, None], 0), axis=1)
    later = chosen & (first[:, None, None, :] < number[None, :, None, None])
    rank = jnp.sum(later.astype(jnp.int32), axis=3)
    slot = expert_list * (CAP * GROUP) + member * CAP + rank
    source = jnp.stack([first, last], axis=2) + member * rows
    source = source.reshape(groups, GROUP, experts, CAP).transpose(0, 2, 1, 3)
    share = gate_probs / jnp.sum(gate_probs, axis=-1, keepdims=True)
    spare = lambda a: jnp.pad(a.reshape(groups, -1), ((0, 1), (0, 0)))
    return spare(source), spare(slot), spare(share)


def local(tokens, norm_gain, gate_weight, up_weight, down_weight, expert_ids, gate_probs):
    section = lax.axis_index("section")
    sections = lax.axis_size("section")
    experts = lax.axis_size("expert")
    micro, rows_one, lanes = tokens.shape
    groups = micro // GROUP
    rows = rows_one * GROUP
    parts = sections
    slots = CAP * GROUP
    turns = sections + groups - 1
    source, slot, share = tables(expert_ids[0], gate_probs[0], experts)
    gain = norm_gain.reshape(parts, lanes)
    w_gate, w_up, w_down = gate_weight[0, 0], up_weight[0, 0], down_weight[0, 0]

    grouped = tokens.reshape(groups, rows, lanes)
    held = jnp.concatenate([grouped[:1], grouped[:0:-1]])
    held = jnp.tile(held, (sections // groups, 1, 1))
    held = lax.all_to_all(held, "section", split_axis=0, concat_axis=0, tiled=True)
    held = held.transpose(1, 0, 2)

    params = pltpu.CompilerParams(vmem_limit_bytes=24 * 1024 * 1024)
    bf = lambda *shape: jax.ShapeDtypeStruct(shape, jnp.bfloat16)
    place = pl.pallas_call(
        place_kernel,
        out_shape=bf(experts, slots, parts, lanes),
        in_specs=[SMEM, SMEM, VMEM, VMEM],
        out_specs=VMEM,
        scratch_shapes=[pltpu.VMEM((rows, parts, lanes), jnp.bfloat16)],
        compiler_params=params,
        name="place",
    )
    expert = pl.pallas_call(
        expert_kernel,
        out_shape=bf(experts * slots, parts, lanes),
        in_specs=[VMEM] * 4,
        out_specs=VMEM,
        scratch_shapes=[pltpu.VMEM((experts * slots * parts, lanes), jnp.float32)],
        compiler_params=params,
        name="expert",
    )
    mix = pl.pallas_call(
        mix_kernel,
        out_shape=bf(rows, parts, lanes),
        in_specs=[SMEM, SMEM, SMEM, VMEM, VMEM],
        out_specs=VMEM,
        compiler_params=params,
        name="mix",
    )
    exchange = lambda a: lax.all_to_all(a, "expert", split_axis=0, concat_axis=0, tiled=True)
    ring = [(i, (i + 1) % sections) for i in range(sections)]

    def layer(turn, held, hidden):
        index = turn - section
        pick = jnp.where((index >= 0) & (index < groups), index, groups).astype(jnp.int32)
        at = pick.reshape(1)
        sent = place(at, source, held, gain)
        arrived = exchange(sent.reshape(experts, slots * parts, lanes))
        results = expert(arrived.reshape(experts * slots, parts, lanes), w_gate, w_up, w_down)
        returned = exchange(results.reshape(experts, slots * parts, lanes))
        output = mix(at, slot, share, returned.reshape(experts * slots, parts, lanes), held)
        return output, lax.dynamic_update_index_in_dim(hidden, output, pick, 0)

    def advance(turn, state):
        output, hidden = layer(turn, *state)
        return lax.ppermute(output, "section", ring), hidden

    hidden = jnp.zeros((groups + 1, rows, parts, lanes), jnp.bfloat16)
    state = lax.fori_loop(0, turns - 1, advance, (held, hidden))
    _, hidden = layer(turns - 1, *state)
    return hidden[:groups].reshape(1, micro, rows_one, parts * lanes)


def solution(mesh):
    in_specs = (
        P(None, "expert", "section"),
        P("section", None),
        P("section", "expert", None, None),
        P("section", "expert", None, None),
        P("section", "expert", None, None),
        P("section", None, "expert", None),
        P("section", None, "expert", None),
    )
    out_specs = P("section", None, "expert", None)
    return jax.shard_map(local, mesh=mesh, in_specs=in_specs, out_specs=out_specs, check_vma=False)
```

time: 1090 us -> 879 us (0.81)
  blocking collectives: 33.3 us -> 315 us
  starting transfers between devices: 310 us -> 126 us
  matrix products: 138 us -> 0 us
  other arithmetic: 124 us -> 4.68 us
  Pallas kernels: 0 us -> 114 us
  local copies, waits for them, and re-layouts: 83.5 us -> 4.94 us
  waiting for transfers between devices: 383 us -> 307 us
    all_to_all x0 -> x19, blocking collectives: none -> 315 us  [local(): lax.all_to_all(a, 'expert', split_axis=0, concat_axis=0, tiled=True)]
    dot_general x92 -> x0, matrix products: 138 us -> none  [the longest x23 40.6 us: expert_block(): jnp.einsum('escd,edf->escf', routed, w_gate, preferred_element_type=jnp.f...]
    all_to_all x46 -> x20, waiting for transfers between devices: 360 us -> 231 us  [the longest x19 221 us: local(): lax.all_to_all(a, 'expert', split_axis=0, concat_axis=0, tiled=True)]
    pallas_call x0 -> x57, Pallas kernels: none -> 114 us  [the longest x19 77.9 us: layer(): expert(arrived.reshape(experts * slots, parts, lanes), w_gate, w_up, w_down)]
    all_to_all x46 -> x20, starting transfers between devices: 203 us -> 91.5 us  [the longest x19 75.7 us: local(): lax.all_to_all(a, 'expert', split_axis=0, concat_axis=0, tiled=True)]
    ppermute x23 -> x18, starting transfers between devices: 107 us -> 35 us  [advance(): return (lax.ppermute(output, 'section', ring), hidden)]
    ppermute x23 -> x18, waiting for transfers between devices: 23 us -> 76.4 us  [advance(): return (lax.ppermute(output, 'section', ring), hidden)]
    convert_element_type x23 -> x0, local copies, waits for them, and re-layouts: 44.2 us -> none  [expert_block(): jnp.einsum('escf,efd->escd', active, w_down, preferred_element_type=jnp.f...]
  transfers between devices with their start and end apart: 69 -> 38, of which waited for: 69 -> 38; matrix products, arithmetic and copies ran while one was open for 5% -> 0% of each run, Pallas kernels for 0% -> 0%
where the time goes in v2:
time: 879 us; the launch traced here: 873 us
  blocking collectives  315 us (36%)
  waiting for transfers between devices  307 us (35%)
  starting transfers between devices  126 us (14%)
  Pallas kernels  114 us (13%)
    all_to_all x19, blocking collectives, local(): lax.all_to_all(a, 'expert', split_axis=0, concat_axis=0, tiled=True)  315 us
    all_to_all x19, waiting for transfers between devices, local(): lax.all_to_all(a, 'expert', split_axis=0, concat_axis=0, tiled=True)  221 us
    pallas_call x19, Pallas kernels, layer(): expert(arrived.reshape(experts * slots, parts, lanes), w_gate, w_up, w_down)  77.9 us
    ppermute x18, waiting for transfers between devices, advance(): return (lax.ppermute(output, 'section', ring), hidden)  76.4 us
    all_to_all x19, starting transfers between devices, local(): lax.all_to_all(a, 'expert', split_axis=0, concat_axis=0, tiled=True)  75.7 us
    ppermute x18, starting transfers between devices, advance(): return (lax.ppermute(output, 'section', ring), hidden)  35 us
    pallas_call x19, Pallas kernels, layer(): sent = place(at, source, held, gain)  20 us
  transfers between devices with their start and end apart: 38, of which 38 were waited for; matrix products, arithmetic and copies ran while one was open for 0% of the time, Pallas kernels for 0%

profile of v2, /device:TPU:1, one launch (start us, length us, event | category | flops | bytes accessed | tf_op | source)
XLA Modules:
  0.0 873.0 jit_solution(6802615773976120469)
XLA Ops:
  5.9 15.7 %all-to-all-start.2 = ((bf16[16,16,128]{2,1,0:T(8,128)(2,1)}), bf16[16,16,128]{2,1,0:T(8,128)(2,1)S(1)}, u32[]{:S(2)}, u32[]{:S(2)}) async-start(bf16[16,16,128]{2,1,0:T(8,128)(2,1)} %bitcast.8), calls=%async_computation.2 | async-start | bytes 131072 | tf_op jit(solution)/shard_map/all_to_all | solution.py:93
  33.3 800.8 %while.15 = (s32[]{:T(128)}, bf16[16,16,128]{2,1,0:T(8,128)(2,1)S(1)}, bf16[5,16,16,128]{3,2,1,0:T(8,128)(2,1)S(1)}, s32[]{:T(128)}, s32[5,128]{1,0:T(8,128)S(1)...) while((s32[]{:T(128)}, ...), condition=%wide.region_6.7_spmd, body=%wide.region_5.6_spmd.sunk | while | flops 10 | bytes 9306437 | solution.py:143
  34.4 20.6 %all_to_all.36 = bf16[32,64,128]{2,1,0:T(8,128)(2,1)S(1)} all-to-all(bf16[32,64,128]{2,1,0:T(8,128)(2,1)S(1)} %bitcast.48), channel_id=1, replica_groups=mesh['section'=16,'expert'=32] {'expert'}, dimensions={0} | all-to-all | bytes 1048576 | tf_op jit(solution)/shard_map/while/body/eval_jaxpr/all_to_all | solution.py:124
  63.0 11.7 %all-to-all-done.1 = bf16[32,64,128]{2,1,0:T(8,128)(2,1)S(1)} async-done(((bf16[32,64,128]{2,1,0:T(8,128)(2,1)}), bf16[32,64,128]{2,1,0:T(8,128)(2,1)S(1)}, u32[]{:S(2)}, u32[]{:S(2)}) %all-to-all-start.1) | async-done | bytes 524320 | tf_op jit(solution)/shard_map/while/body/eval_jaxpr/all_to_all | solution.py:124
  82.8 16.4 %all_to_all.36 = bf16[32,64,128]{2,1,0:T(8,128)(2,1)S(1)} all-to-all(bf16[32,64,128]{2,1,0:T(8,128)(2,1)S(1)} %bitcast.48), channel_id=1, replica_groups=mesh['section'=16,'expert'=32] {'expert'}, dimensions={0} | all-to-all | bytes 1048576 | tf_op jit(solution)/shard_map/while/body/eval_jaxpr/all_to_all | solution.py:124
  107.3 11.7 %all-to-all-done.1 = bf16[32,64,128]{2,1,0:T(8,128)(2,1)S(1)} async-done(((bf16[32,64,128]{2,1,0:T(8,128)(2,1)}), bf16[32,64,128]{2,1,0:T(8,128)(2,1)S(1)}, u32[]{:S(2)}, u32[]{:S(2)}) %all-to-all-start.1) | async-done | bytes 524320 | tf_op jit(solution)/shard_map/while/body/eval_jaxpr/all_to_all | solution.py:124
  127.1 16.4 %all_to_all.36 = bf16[32,64,128]{2,1,0:T(8,128)(2,1)S(1)} all-to-all(bf16[32,64,128]{2,1,0:T(8,128)(2,1)S(1)} %bitcast.48), channel_id=1, replica_groups=mesh['section'=16,'expert'=32] {'expert'}, dimensions={0} | all-to-all | bytes 1048576 | tf_op jit(solution)/shard_map/while/body/eval_jaxpr/all_to_all | solution.py:124
  151.6 11.7 %all-to-all-done.1 = bf16[32,64,128]{2,1,0:T(8,128)(2,1)S(1)} async-done(((bf16[32,64,128]{2,1,0:T(8,128)(2,1)}), bf16[32,64,128]{2,1,0:T(8,128)(2,1)S(1)}, u32[]{:S(2)}, u32[]{:S(2)}) %all-to-all-start.1) | async-done | bytes 524320 | tf_op jit(solution)/shard_map/while/body/eval_jaxpr/all_to_all | solution.py:124
  171.3 16.4 %all_to_all.36 = bf16[32,64,128]{2,1,0:T(8,128)(2,1)S(1)} all-to-all(bf16[32,64,128]{2,1,0:T(8,128)(2,1)S(1)} %bitcast.48), channel_id=1, replica_groups=mesh['section'=16,'expert'=32] {'expert'}, dimensions={0} | all-to-all | bytes 1048576 | tf_op jit(solution)/shard_map/while/body/eval_jaxpr/all_to_all | solution.py:124
  195.8 11.7 %all-to-all-done.1 = bf16[32,64,128]{2,1,0:T(8,128)(2,1)S(1)} async-done(((bf16[32,64,128]{2,1,0:T(8,128)(2,1)}), bf16[32,64,128]{2,1,0:T(8,128)(2,1)S(1)}, u32[]{:S(2)}, u32[]{:S(2)}) %all-to-all-start.1) | async-done | bytes 524320 | tf_op jit(solution)/shard_map/while/body/eval_jaxpr/all_to_all | solution.py:124
  215.6 16.4 %all_to_all.36 = bf16[32,64,128]{2,1,0:T(8,128)(2,1)S(1)} all-to-all(bf16[32,64,128]{2,1,0:T(8,128)(2,1)S(1)} %bitcast.48), channel_id=1, replica_groups=mesh['section'=16,'expert'=32] {'expert'}, dimensions={0} | all-to-all | bytes 1048576 | tf_op jit(solution)/shard_map/while/body/eval_jaxpr/all_to_all | solution.py:124
  240.1 11.7 %all-to-all-done.1 = bf16[32,64,128]{2,1,0:T(8,128)(2,1)S(1)} async-done(((bf16[32,64,128]{2,1,0:T(8,128)(2,1)}), bf16[32,64,128]{2,1,0:T(8,128)(2,1)S(1)}, u32[]{:S(2)}, u32[]{:S(2)}) %all-to-all-start.1) | async-done | bytes 524320 | tf_op jit(solution)/shard_map/while/body/eval_jaxpr/all_to_all | solution.py:124
  259.8 16.4 %all_to_all.36 = bf16[32,64,128]{2,1,0:T(8,128)(2,1)S(1)} all-to-all(bf16[32,64,128]{2,1,0:T(8,128)(2,1)S(1)} %bitcast.48), channel_id=1, replica_groups=mesh['section'=16,'expert'=32] {'expert'}, dimensions={0} | all-to-all | bytes 1048576 | tf_op jit(solution)/shard_map/while/body/eval_jaxpr/all_to_all | solution.py:124
  304.1 16.4 %all_to_all.36 = bf16[32,64,128]{2,1,0:T(8,128)(2,1)S(1)} all-to-all(bf16[32,64,128]{2,1,0:T(8,128)(2,1)S(1)} %bitcast.48), channel_id=1, replica_groups=mesh['section'=16,'expert'=32] {'expert'}, dimensions={0} | all-to-all | bytes 1048576 | tf_op jit(solution)/shard_map/while/body/eval_jaxpr/all_to_all | solution.py:124
  328.6 11.7 %all-to-all-done.1 = bf16[32,64,128]{2,1,0:T(8,128)(2,1)S(1)} async-done(((bf16[32,64,128]{2,1,0:T(8,128)(2,1)}), bf16[32,64,128]{2,1,0:T(8,128)(2,1)S(1)}, u32[]{:S(2)}, u32[]{:S(2)}) %all-to-all-start.1) | async-done | bytes 524320 | tf_op jit(solution)/shard_map/while/body/eval_jaxpr/all_to_all | solution.py:124
  348.4 16.4 %all_to_all.36 = bf16[32,64,128]{2,1,0:T(8,128)(2,1)S(1)} all-to-all(bf16[32,64,128]{2,1,0:T(8,128)(2,1)S(1)} %bitcast.48), channel_id=1, replica_groups=mesh['section'=16,'expert'=32] {'expert'}, dimensions={0} | all-to-all | bytes 1048576 | tf_op jit(solution)/shard_map/while/body/eval_jaxpr/all_to_all | solution.py:124
  372.8 11.7 %all-to-all-done.1 = bf16[32,64,128]{2,1,0:T(8,128)(2,1)S(1)} async-done(((bf16[32,64,128]{2,1,0:T(8,128)(2,1)}), bf16[32,64,128]{2,1,0:T(8,128)(2,1)S(1)}, u32[]{:S(2)}, u32[]{:S(2)}) %all-to-all-start.1) | async-done | bytes 524320 | tf_op jit(solution)/shard_map/while/body/eval_jaxpr/all_to_all | solution.py:124
  392.6 16.4 %all_to_all.36 = bf16[32,64,128]{2,1,0:T(8,128)(2,1)S(1)} all-to-all(bf16[32,64,128]{2,1,0:T(8,128)(2,1)S(1)} %bitcast.48), channel_id=1, replica_groups=mesh['section'=16,'expert'=32] {'expert'}, dimensions={0} | all-to-all | bytes 1048576 | tf_op jit(solution)/shard_map/while/body/eval_jaxpr/all_to_all | solution.py:124
  436.9 16.4 %all_to_all.36 = bf16[32,64,128]{2,1,0:T(8,128)(2,1)S(1)} all-to-all(bf16[32,64,128]{2,1,0:T(8,128)(2,1)S(1)} %bitcast.48), channel_id=1, replica_groups=mesh['section'=16,'expert'=32] {'expert'}, dimensions={0} | all-to-all | bytes 1048576 | tf_op jit(solution)/shard_map/while/body/eval_jaxpr/all_to_all | solution.py:124
  461.4 11.7 %all-to-all-done.1 = bf16[32,64,128]{2,1,0:T(8,128)(2,1)S(1)} async-done(((bf16[32,64,128]{2,1,0:T(8,128)(2,1)}), bf16[32,64,128]{2,1,0:T(8,128)(2,1)S(1)}, u32[]{:S(2)}, u32[]{:S(2)}) %all-to-all-start.1) | async-done | bytes 524320 | tf_op jit(solution)/shard_map/while/body/eval_jaxpr/all_to_all | solution.py:124
  481.1 16.4 %all_to_all.36 = bf16[32,64,128]{2,1,0:T(8,128)(2,1)S(1)} all-to-all(bf16[32,64,128]{2,1,0:T(8,128)(2,1)S(1)} %bitcast.48), channel_id=1, replica_groups=mesh['section'=16,'expert'=32] {'expert'}, dimensions={0} | all-to-all | bytes 1048576 | tf_op jit(solution)/shard_map/while/body/eval_jaxpr/all_to_all | solution.py:124
  505.6 11.7 %all-to-all-done.1 = bf16[32,64,128]{2,1,0:T(8,128)(2,1)S(1)} async-done(((bf16[32,64,128]{2,1,0:T(8,128)(2,1)}), bf16[32,64,128]{2,1,0:T(8,128)(2,1)S(1)}, u32[]{:S(2)}, u32[]{:S(2)}) %all-to-all-start.1) | async-done | bytes 524320 | tf_op jit(solution)/shard_map/while/body/eval_jaxpr/all_to_all | solution.py:124
  525.4 16.4 %all_to_all.36 = bf16[32,64,128]{2,1,0:T(8,128)(2,1)S(1)} all-to-all(bf16[32,64,128]{2,1,0:T(8,128)(2,1)S(1)} %bitcast.48), channel_id=1, replica_groups=mesh['section'=16,'expert'=32] {'expert'}, dimensions={0} | all-to-all | bytes 1048576 | tf_op jit(solution)/shard_map/while/body/eval_jaxpr/all_to_all | solution.py:124
  549.9 11.7 %all-to-all-done.1 = bf16[32,64,128]{2,1,0:T(8,128)(2,1)S(1)} async-done(((bf16[32,64,128]{2,1,0:T(8,128)(2,1)}), bf16[32,64,128]{2,1,0:T(8,128)(2,1)S(1)}, u32[]{:S(2)}, u32[]{:S(2)}) %all-to-all-start.1) | async-done | bytes 524320 | tf_op jit(solution)/shard_map/while/body/eval_jaxpr/all_to_all | solution.py:124
  569.6 16.4 %all_to_all.36 = bf16[32,64,128]{2,1,0:T(8,128)(2,1)S(1)} all-to-all(bf16[32,64,128]{2,1,0:T(8,128)(2,1)S(1)} %bitcast.48), channel_id=1, replica_groups=mesh['section'=16,'expert'=32] {'expert'}, dimensions={0} | all-to-all | bytes 1048576 | tf_op jit(solution)/shard_map/while/body/eval_jaxpr/all_to_all | solution.py:124
  613.9 16.4 %all_to_all.36 = bf16[32,64,128]{2,1,0:T(8,128)(2,1)S(1)} all-to-all(bf16[32,64,128]{2,1,0:T(8,128)(2,1)S(1)} %bitcast.48), channel_id=1, replica_groups=mesh['section'=16,'expert'=32] {'expert'}, dimensions={0} | all-to-all | bytes 1048576 | tf_op jit(solution)/shard_map/while/body/eval_jaxpr/all_to_all | solution.py:124
  658.2 16.4 %all_to_all.36 = bf16[32,64,128]{2,1,0:T(8,128)(2,1)S(1)} all-to-all(bf16[32,64,128]{2,1,0:T(8,128)(2,1)S(1)} %bitcast.48), channel_id=1, replica_groups=mesh['section'=16,'expert'=32] {'expert'}, dimensions={0} | all-to-all | bytes 1048576 | tf_op jit(solution)/shard_map/while/body/eval_jaxpr/all_to_all | solution.py:124
  702.4 16.4 %all_to_all.36 = bf16[32,64,128]{2,1,0:T(8,128)(2,1)S(1)} all-to-all(bf16[32,64,128]{2,1,0:T(8,128)(2,1)S(1)} %bitcast.48), channel_id=1, replica_groups=mesh['section'=16,'expert'=32] {'expert'}, dimensions={0} | all-to-all | bytes 1048576 | tf_op jit(solution)/shard_map/while/body/eval_jaxpr/all_to_all | solution.py:124
  746.7 16.4 %all_to_all.36 = bf16[32,64,128]{2,1,0:T(8,128)(2,1)S(1)} all-to-all(bf16[32,64,128]{2,1,0:T(8,128)(2,1)S(1)} %bitcast.48), channel_id=1, replica_groups=mesh['section'=16,'expert'=32] {'expert'}, dimensions={0} | all-to-all | bytes 1048576 | tf_op jit(solution)/shard_map/while/body/eval_jaxpr/all_to_all | solution.py:124
  790.9 16.4 %all_to_all.36 = bf16[32,64,128]{2,1,0:T(8,128)(2,1)S(1)} all-to-all(bf16[32,64,128]{2,1,0:T(8,128)(2,1)S(1)} %bitcast.48), channel_id=1, replica_groups=mesh['section'=16,'expert'=32] {'expert'}, dimensions={0} | all-to-all | bytes 1048576 | tf_op jit(solution)/shard_map/while/body/eval_jaxpr/all_to_all | solution.py:124
  835.2 16.4 %all_to_all.35 = bf16[32,64,128]{2,1,0:T(8,128)(2,1)S(1)} all-to-all(bf16[32,64,128]{2,1,0:T(8,128)(2,1)S(1)} %bitcast.51), channel_id=1, replica_groups=mesh['section'=16,'expert'=32] {'expert'}, dimensions={0} | all-to-all | bytes 1048576 | tf_op jit(solution)/shard_map/all_to_all | solution.py:124
  859.7 11.7 %all-to-all-done.4 = bf16[32,64,128]{2,1,0:T(8,128)(2,1)S(1)} async-done(((bf16[32,64,128]{2,1,0:T(8,128)(2,1)}), bf16[32,64,128]{2,1,0:T(8,128)(2,1)S(1)}, u32[]{:S(2)}, u32[]{:S(2)}) %all-to-all-start.4) | async-done | bytes 524320 | tf_op jit(solution)/shard_map/all_to_all | solution.py:124
  (210 shorter events, 412.9 us)
Async XLA Ops:
  5.9 27.3 %all-to-all-start.2 = ((bf16[16,16,128]{2,1,0:T(8,128)(2,1)}), bf16[16,16,128]{2,1,0:T(8,128)(2,1)S(1)}, u32[]{:S(2)}, u32[]{:S(2)}) async-start(bf16[16,16,128]{2,1,0:T(8,128)(2,1)} %bitcast.8), calls=%async_computation.2 | async-start | bytes 131072 | tf_op jit(solution)/shard_map/all_to_all | solution.py:93
  59.0 15.7 %all-to-all-start.1 = ((bf16[32,64,128]{2,1,0:T(8,128)(2,1)}), bf16[32,64,128]{2,1,0:T(8,128)(2,1)S(1)}, u32[]{:S(2)}, u32[]{:S(2)}) async-start(bf16[32,64,128]{2,1,0:T(8,128)(2,1)} %bitcast.45), calls=%async_computation.1 | async-start | bytes 1048576 | tf_op jit(solution)/shard_map/while/body/eval_jaxpr/all_to_all | solution.py:124
  75.5 6.2 collective-permute-start
  103.3 15.7 %all-to-all-start.1 = ((bf16[32,64,128]{2,1,0:T(8,128)(2,1)}), bf16[32,64,128]{2,1,0:T(8,128)(2,1)S(1)}, u32[]{:S(2)}, u32[]{:S(2)}) async-start(bf16[32,64,128]{2,1,0:T(8,128)(2,1)} %bitcast.45), calls=%async_computation.1 | async-start | bytes 1048576 | tf_op jit(solution)/shard_map/while/body/eval_jaxpr/all_to_all | solution.py:124
  119.8 6.2 collective-permute-start
  147.5 15.7 %all-to-all-start.1 = ((bf16[32,64,128]{2,1,0:T(8,128)(2,1)}), bf16[32,64,128]{2,1,0:T(8,128)(2,1)S(1)}, u32[]{:S(2)}, u32[]{:S(2)}) async-start(bf16[32,64,128]{2,1,0:T(8,128)(2,1)} %bitcast.45), calls=%async_computation.1 | async-start | bytes 1048576 | tf_op jit(solution)/shard_map/while/body/eval_jaxpr/all_to_all | solution.py:124
  164.0 6.2 collective-permute-start
  191.8 15.7 %all-to-all-start.1 = ((bf16[32,64,128]{2,1,0:T(8,128)(2,1)}), bf16[32,64,128]{2,1,0:T(8,128)(2,1)S(1)}, u32[]{:S(2)}, u32[]{:S(2)}) async-start(bf16[32,64,128]{2,1,0:T(8,128)(2,1)} %bitcast.45), calls=%async_computation.1 | async-start | bytes 1048576 | tf_op jit(solution)/shard_map/while/body/eval_jaxpr/all_to_all | solution.py:124
  208.3 6.2 collective-permute-start
  236.1 15.7 %all-to-all-start.1 = ((bf16[32,64,128]{2,1,0:T(8,128)(2,1)}), bf16[32,64,128]{2,1,0:T(8,128)(2,1)S(1)}, u32[]{:S(2)}, u32[]{:S(2)}) async-start(bf16[32,64,128]{2,1,0:T(8,128)(2,1)} %bitcast.45), calls=%async_computation.1 | async-start | bytes 1048576 | tf_op jit(solution)/shard_map/while/body/eval_jaxpr/all_to_all | solution.py:124
  252.6 6.2 collective-permute-start
  280.3 15.7 %all-to-all-start.1 = ((bf16[32,64,128]{2,1,0:T(8,128)(2,1)}), bf16[32,64,128]{2,1,0:T(8,128)(2,1)S(1)}, u32[]{:S(2)}, u32[]{:S(2)}) async-start(bf16[32,64,128]{2,1,0:T(8,128)(2,1)} %bitcast.45), calls=%async_computation.1 | async-start | bytes 1048576 | tf_op jit(solution)/shard_map/while/body/eval_jaxpr/all_to_all | solution.py:124
  296.8 6.2 collective-permute-start
  324.6 15.7 %all-to-all-start.1 = ((bf16[32,64,128]{2,1,0:T(8,128)(2,1)}), bf16[32,64,128]{2,1,0:T(8,128)(2,1)S(1)}, u32[]{:S(2)}, u32[]{:S(2)}) async-start(bf16[32,64,128]{2,1,0:T(8,128)(2,1)} %bitcast.45), calls=%async_computation.1 | async-start | bytes 1048576 | tf_op jit(solution)/shard_map/while/body/eval_jaxpr/all_to_all | solution.py:124
  341.1 6.2 collective-permute-start
  368.8 15.7 %all-to-all-start.1 = ((bf16[32,64,128]{2,1,0:T(8,128)(2,1)}), bf16[32,64,128]{2,1,0:T(8,128)(2,1)S(1)}, u32[]{:S(2)}, u32[]{:S(2)}) async-start(bf16[32,64,128]{2,1,0:T(8,128)(2,1)} %bitcast.45), calls=%async_computation.1 | async-start | bytes 1048576 | tf_op jit(solution)/shard_map/while/body/eval_jaxpr/all_to_all | solution.py:124
  385.3 6.2 collective-permute-start
  413.1 15.7 %all-to-all-start.1 = ((bf16[32,64,128]{2,1,0:T(8,128)(2,1)}), bf16[32,64,128]{2,1,0:T(8,128)(2,1)S(1)}, u32[]{:S(2)}, u32[]{:S(2)}) async-start(bf16[32,64,128]{2,1,0:T(8,128)(2,1)} %bitcast.45), calls=%async_computation.1 | async-start | bytes 1048576 | tf_op jit(solution)/shard_map/while/body/eval_jaxpr/all_to_all | solution.py:124
  429.6 6.2 collective-permute-start
  457.3 15.7 %all-to-all-start.1 = ((bf16[32,64,128]{2,1,0:T(8,128)(2,1)}), bf16[32,64,128]{2,1,0:T(8,128)(2,1)S(1)}, u32[]{:S(2)}, u32[]{:S(2)}) async-start(bf16[32,64,128]{2,1,0:T(8,128)(2,1)} %bitcast.45), calls=%async_computation.1 | async-start | bytes 1048576 | tf_op jit(solution)/shard_map/while/body/eval_jaxpr/all_to_all | solution.py:124
  473.8 6.2 collective-permute-start
  501.6 15.7 %all-to-all-start.1 = ((bf16[32,64,128]{2,1,0:T(8,128)(2,1)}), bf16[32,64,128]{2,1,0:T(8,128)(2,1)S(1)}, u32[]{:S(2)}, u32[]{:S(2)}) async-start(bf16[32,64,128]{2,1,0:T(8,128)(2,1)} %bitcast.45), calls=%async_computation.1 | async-start | bytes 1048576 | tf_op jit(solution)/shard_map/while/body/eval_jaxpr/all_to_all | solution.py:124
  545.9 15.7 %all-to-all-start.1 = ((bf16[32,64,128]{2,1,0:T(8,128)(2,1)}), bf16[32,64,128]{2,1,0:T(8,128)(2,1)S(1)}, u32[]{:S(2)}, u32[]{:S(2)}) async-start(bf16[32,64,128]{2,1,0:T(8,128)(2,1)} %bitcast.45), calls=%async_computation.1 | async-start | bytes 1048576 | tf_op jit(solution)/shard_map/while/body/eval_jaxpr/all_to_all | solution.py:124
  590.1 15.7 %all-to-all-start.1 = ((bf16[32,64,128]{2,1,0:T(8,128)(2,1)}), bf16[32,64,128]{2,1,0:T(8,128)(2,1)S(1)}, u32[]{:S(2)}, u32[]{:S(2)}) async-start(bf16[32,64,128]{2,1,0:T(8,128)(2,1)} %bitcast.45), calls=%async_computation.1 | async-start | bytes 1048576 | tf_op jit(solution)/shard_map/while/body/eval_jaxpr/all_to_all | solution.py:124
  634.4 15.7 %all-to-all-start.1 = ((bf16[32,64,128]{2,1,0:T(8,128)(2,1)}), bf16[32,64,128]{2,1,0:T(8,128)(2,1)S(1)}, u32[]{:S(2)}, u32[]{:S(2)}) async-start(bf16[32,64,128]{2,1,0:T(8,128)(2,1)} %bitcast.45), calls=%async_computation.1 | async-start | bytes 1048576 | tf_op jit(solution)/shard_map/while/body/eval_jaxpr/all_to_all | solution.py:124
  678.6 15.7 %all-to-all-start.1 = ((bf16[32,64,128]{2,1,0:T(8,128)(2,1)}), bf16[32,64,128]{2,1,0:T(8,128)(2,1)S(1)}, u32[]{:S(2)}, u32[]{:S(2)}) async-start(bf16[32,64,128]{2,1,0:T(8,128)(2,1)} %bitcast.45), calls=%async_computation.1 | async-start | bytes 1048576 | tf_op jit(solution)/shard_map/while/body/eval_jaxpr/all_to_all | solution.py:124
  722.9 15.7 %all-to-all-start.1 = ((bf16[32,64,128]{2,1,0:T(8,128)(2,1)}), bf16[32,64,128]{2,1,0:T(8,128)(2,1)S(1)}, u32[]{:S(2)}, u32[]{:S(2)}) async-start(bf16[32,64,128]{2,1,0:T(8,128)(2,1)} %bitcast.45), calls=%async_computation.1 | async-start | bytes 1048576 | tf_op jit(solution)/shard_map/while/body/eval_jaxpr/all_to_all | solution.py:124
  739.4 6.2 collective-permute-start
  767.1 15.7 %all-to-all-start.1 = ((bf16[32,64,128]{2,1,0:T(8,128)(2,1)}), bf16[32,64,128]{2,1,0:T(8,128)(2,1)S(1)}, u32[]{:S(2)}, u32[]{:S(2)}) async-start(bf16[32,64,128]{2,1,0:T(8,128)(2,1)} %bitcast.45), calls=%async_computation.1 | async-start | bytes 1048576 | tf_op jit(solution)/shard_map/while/body/eval_jaxpr/all_to_all | solution.py:124
  783.6 6.2 collective-permute-start
  811.4 15.7 %all-to-all-start.1 = ((bf16[32,64,128]{2,1,0:T(8,128)(2,1)}), bf16[32,64,128]{2,1,0:T(8,128)(2,1)S(1)}, u32[]{:S(2)}, u32[]{:S(2)}) async-start(bf16[32,64,128]{2,1,0:T(8,128)(2,1)} %bitcast.45), calls=%async_computation.1 | async-start | bytes 1048576 | tf_op jit(solution)/shard_map/while/body/eval_jaxpr/all_to_all | solution.py:124
  855.7 15.7 %all-to-all-start.4 = ((bf16[32,64,128]{2,1,0:T(8,128)(2,1)}), bf16[32,64,128]{2,1,0:T(8,128)(2,1)S(1)}, u32[]{:S(2)}, u32[]{:S(2)}) async-start(bf16[32,64,128]{2,1,0:T(8,128)(2,1)} %bitcast.22), calls=%async_computation.4 | async-start | bytes 1048576 | tf_op jit(solution)/shard_map/all_to_all | solution.py:124
  (25 other events, 372.8 us)

commit v3 on v2

--- a/solution.py
+++ b/solution.py
@@ -1,3 +1,5 @@
+import functools
+
 import jax
 import jax.numpy as jnp
 from jax import lax
@@ -12,6 +14,7 @@
 
 VMEM = pl.BlockSpec(memory_space=pltpu.VMEM)
 SMEM = pl.BlockSpec(memory_space=pltpu.SMEM)
+ANY = pl.BlockSpec(memory_space=pl.ANY)
 
 
 def place_kernel(turn_ref, row_ref, x_ref, gain_ref, send_ref, normed_ref):
@@ -26,16 +29,37 @@
             send_ref[e, q] = normed_ref[row_ref[pick, e * slots + q]]
 
 
-def expert_kernel(recv_ref, gate_ref, up_ref, down_ref, out_ref, wide_ref):
+def expert_kernel(own_ref, recv_ref, *refs):
+    out_ref, gate_ref, up_ref, down_ref, wide_ref, sems = refs[-6:]
+    weights, held = refs[:-6], (gate_ref, up_ref, down_ref)
     rows, parts, lanes = recv_ref.shape
+    copies = [pltpu.make_async_copy(weights[i], held[i], sems.at[i]) for i in range(3)]
+    if len(weights) == 3:
+        for copy in copies:
+            copy.start()
+    else:
+
+        @pl.when(own_ref[0] == 1)
+        def _():
+            for copy in copies:
+                copy.start()
+
+        @pl.when(own_ref[0] != 1)
+        def _():
+            for i in range(3):
+                pltpu.make_async_copy(weights[3 + i], held[i], sems.at[i]).start()
+
     wide_ref[...] = recv_ref[...].astype(jnp.float32).reshape(rows * parts, lanes)
     routed = jnp.concatenate(
         [wide_ref[pl.ds(c, rows, stride=parts), :].astype(jnp.bfloat16) for c in range(parts)],
         axis=1,
     )
+    copies[0].wait()
     gate = jnp.dot(routed, gate_ref[...], preferred_element_type=jnp.float32)
+    copies[1].wait()
     up = jnp.dot(routed, up_ref[...], preferred_element_type=jnp.float32)
     active = (gate / (1.0 + jnp.exp(-gate)) * up).astype(jnp.bfloat16)
+    copies[2].wait()
     result = jnp.dot(active, down_ref[...], preferred_element_type=jnp.float32)
     for c in range(parts):
         wide_ref[pl.ds(c, rows, stride=parts), :] = result[:, c * lanes : (c + 1) * lanes]
@@ -77,21 +101,35 @@
     section = lax.axis_index("section")
     sections = lax.axis_size("section")
     experts = lax.axis_size("expert")
+    column, stage = section % 2, section // 2
     micro, rows_one, lanes = tokens.shape
     groups = micro // GROUP
     rows = rows_one * GROUP
     parts = sections
     slots = CAP * GROUP
-    turns = sections + groups - 1
+    last = sections + groups - 2
+    swap = [(i, i ^ 1) for i in range(sections)]
+
+    fresh = jnp.broadcast_to(tokens.reshape(1, -1, lanes), (sections, micro * rows_one, lanes))
+    fresh = lax.all_to_all(fresh, "section", split_axis=0, concat_axis=0, tiled=True)
+    fresh = fresh.transpose(1, 0, 2).reshape(groups, rows, parts, lanes)
+
     source, slot, share = tables(expert_ids[0], gate_probs[0], experts)
     gain = norm_gain.reshape(parts, lanes)
-    w_gate, w_up, w_down = gate_weight[0, 0], up_weight[0, 0], down_weight[0, 0]
-
-    grouped = tokens.reshape(groups, rows, lanes)
-    held = jnp.concatenate([grouped[:1], grouped[:0:-1]])
-    held = jnp.tile(held, (sections // groups, 1, 1))
-    held = lax.all_to_all(held, "section", split_axis=0, concat_axis=0, tiled=True)
-    held = held.transpose(1, 0, 2)
+    flat = lambda a: a.reshape(-1, lanes).astype(jnp.float32)
+    packed = jnp.concatenate([flat(source), flat(slot), flat(share), gain])
+    moved = lax.ppermute(packed, "section", swap)
+    both = jnp.where(column == 0, jnp.stack([packed, moved]), jnp.stack([moved, packed]))
+    size = source.size // lanes
+    as_table = lambda a: a.reshape(2 * (groups + 1), -1)
+    source = as_table(both[:, :size]).astype(jnp.int32)
+    slot = as_table(both[:, size : 2 * size]).astype(jnp.int32)
+    share = as_table(both[:, 2 * size : 3 * size])
+    gains = both[:, 3 * size :].reshape(2 * parts, lanes)
+
+    own_weights = (gate_weight[0, 0], up_weight[0, 0], down_weight[0, 0])
+    ready, fresh, gains = lax.optimization_barrier((own_weights, fresh, gains))
+    other_weights = tuple(lax.ppermute(w, "section", swap[2:]) for w in ready)
 
     params = pltpu.CompilerParams(vmem_limit_bytes=24 * 1024 * 1024)
     bf = lambda *shape: jax.ShapeDtypeStruct(shape, jnp.bfloat16)
@@ -104,15 +142,21 @@
         compiler_params=params,
         name="place",
     )
-    expert = pl.pallas_call(
-        expert_kernel,
-        out_shape=bf(experts * slots, parts, lanes),
-        in_specs=[VMEM] * 4,
-        out_specs=VMEM,
-        scratch_shapes=[pltpu.VMEM((experts * slots * parts, lanes), jnp.float32)],
-        compiler_params=params,
-        name="expert",
-    )
+    def expert(own, arrived, *weights):
+        return pl.pallas_call(
+            expert_kernel,
+            out_shape=bf(experts * slots, parts, lanes),
+            in_specs=[SMEM, VMEM] + [ANY] * len(weights),
+            out_specs=VMEM,
+            scratch_shapes=[pltpu.VMEM(w.shape, jnp.bfloat16) for w in own_weights]
+            + [
+                pltpu.VMEM((experts * slots * parts, lanes), jnp.float32),
+                pltpu.SemaphoreType.DMA((3,)),
+            ],
+            compiler_params=params,
+            name="expert",
+        )(own, arrived, *weights)
+
     mix = pl.pallas_call(
         mix_kernel,
         out_shape=bf(rows, parts, lanes),
@@ -122,27 +166,79 @@
         name="mix",
     )
     exchange = lambda a: lax.all_to_all(a, "expert", split_axis=0, concat_axis=0, tiled=True)
-    ring = [(i, (i + 1) % sections) for i in range(sections)]
-
-    def layer(turn, held, hidden):
-        index = turn - section
-        pick = jnp.where((index >= 0) & (index < groups), index, groups).astype(jnp.int32)
+
+    def layer(turn, held, hidden, weights):
+        second = jnp.where(stage == 0, column, (turn - column) % 2)
+        group = turn - 2 * stage - second
+        active = (group >= 0) & (group < groups)
+        pick = (jnp.where(active, group, groups) + second * (groups + 1)).astype(jnp.int32)
+        own = ((stage == 0) | (second == column)).astype(jnp.int32).reshape(1)
         at = pick.reshape(1)
-        sent = place(at, source, held, gain)
+        gain_now = lax.dynamic_slice_in_dim(gains, second * parts, parts, 0)
+        sent = place(at, source, held, gain_now)
         arrived = exchange(sent.reshape(experts, slots * parts, lanes))
-        results = expert(arrived.reshape(experts * slots, parts, lanes), w_gate, w_up, w_down)
+        results = expert(own, arrived.reshape(experts * slots, parts, lanes), *weights)
         returned = exchange(results.reshape(experts, slots * parts, lanes))
         output = mix(at, slot, share, returned.reshape(experts * slots, parts, lanes), held)
         return output, lax.dynamic_update_index_in_dim(hidden, output, pick, 0)
 
-    def advance(turn, state):
-        output, hidden = layer(turn, *state)
-        return lax.ppermute(output, "section", ring), hidden
-
-    hidden = jnp.zeros((groups + 1, rows, parts, lanes), jnp.bfloat16)
-    state = lax.fori_loop(0, turns - 1, advance, (held, hidden))
-    _, hidden = layer(turns - 1, *state)
-    return hidden[:groups].reshape(1, micro, rows_one, parts * lanes)
+    def move(value, pairs):
+        here = functools.reduce(jnp.logical_or, [section == b for _, b in pairs])
+        return jnp.where(here, lax.ppermute(value, "section", pairs), value)
+
+    def opening_pairs(turn):
+        pairs = [(0, 1)] if turn < groups else []
+        pairs += [(1, 2 + (turn - 1) % 2)] if 1 <= turn <= groups else []
+        for a in range(2, sections - 2):
+            group = turn - (a // 2 * 2 + 1)
+            if 0 <= group < groups and group % 2 == a % 2:
+                pairs.append((a, a + 2))
+        return pairs
+
+    def steady_pairs(parity):
+        return [(a, a + 2) for a in range(2 + parity, sections - 2, 2)]
+
+    hidden = jnp.zeros((2 * (groups + 1), rows, parts, lanes), jnp.bfloat16)
+    held = jnp.zeros((rows, parts, lanes), jnp.bfloat16)
+
+    def entering(turn, held):
+        group = lax.dynamic_index_in_dim(fresh, turn, 0, keepdims=False)
+        return jnp.where(section == 0, group, held)
+
+    def begin(turn, state):
+        held, hidden = state
+        held, hidden = layer(turn, entering(turn, held), hidden, own_weights)
+        return move(held, opening_pairs(0) + opening_pairs(1)[1:]), hidden
+
+    held, hidden = lax.fori_loop(0, 2, begin, (held, hidden))
+    held, other_weights = lax.optimization_barrier((held, other_weights))
+    all_weights = own_weights + other_weights
+    for turn in range(2, groups + 1):
+        if turn < groups:
+            held = entering(turn, held)
+        held, hidden = layer(turn, held, hidden, own_weights if turn < 3 else all_weights)
+        held = move(held, opening_pairs(turn))
+
+    def advance(i, state):
+        held, hidden = state
+        for step in range(2):
+            turn = groups + 1 + 2 * i + step
+            held, hidden = layer(turn, held, hidden, all_weights)
+            held = move(held, steady_pairs((groups + 2 + step) % 2))
+        return held, hidden
+
+    held, hidden = lax.fori_loop(0, (last - 2 - groups) // 2, advance, (held, hidden))
+    for turn in (last - 1, last):
+        held, hidden = layer(turn, held, hidden, all_weights)
+
+    low, high = hidden[:groups], hidden[groups + 1 : 2 * groups + 1]
+    theirs = jnp.where(column == 0, high[0::2], low[1::2])
+    theirs = lax.ppermute(theirs, "section", swap)
+    mine = jnp.where(column == 0, low, high)
+    result = [
+        jnp.where((stage == 0) | (column == j % 2), mine[j], theirs[j // 2]) for j in range(groups)
+    ]
+    return jnp.stack(result).reshape(1, micro, rows_one, parts * lanes)
 
 
 def solution(mesh):

time: 879 us -> 856 us (0.974)
  the two profiles are of different devices: /device:TPU:1 before, /device:TPU:64 now
where the time goes in v3:
time: 856 us; the launch traced here: 850 us
  waiting for transfers between devices  398 us (46%)
  starting transfers between devices  204 us (24%)
  blocking collectives  122 us (14%)
  Pallas kernels  113 us (13%)
    all_to_all x30, waiting for transfers between devices, local(): lax.all_to_all(a, 'expert', split_axis=0, concat_axis=0, tiled=True)  352 us
    all_to_all x30, starting transfers between devices, local(): lax.all_to_all(a, 'expert', split_axis=0, concat_axis=0, tiled=True)  124 us
    all_to_all x8, blocking collectives, local(): lax.all_to_all(a, 'expert', split_axis=0, concat_axis=0, tiled=True)  122 us
    pallas_call x19, Pallas kernels, expert(): pl.pallas_call(expert_kernel, out_shape=bf(experts * slots, parts, lanes)...  62.3 us
    ppermute x17, starting transfers between devices, move(): return jnp.where(here, lax.ppermute(value, 'section', pairs), value)  45 us
    pallas_call x19, Pallas kernels, layer(): sent = place(at, source, held, gain_now)  32.3 us
    ppermute x17, waiting for transfers between devices, move(): return jnp.where(here, lax.ppermute(value, 'section', pairs), value)  27.9 us
    pallas_call x19, Pallas kernels, layer(): mix(at, slot, share, returned.reshape(experts * slots, parts, lanes), held)  18.5 us
  transfers between devices with their start and end apart: 53, of which 43 were waited for; matrix products, arithmetic and copies ran while one was open for 0% of the time, Pallas kernels for 2%

profile of v3, /device:TPU:64, one launch (start us, length us, event | category | flops | bytes accessed | tf_op | source)
XLA Modules:
  0.0 850.4 jit_solution(17354346106369387288)
XLA Ops:
  5.6 14.8 %all-to-all-start.6 = ((bf16[16,64,128]{2,1,0:T(8,128)(2,1)}), bf16[16,64,128]{2,1,0:T(8,128)(2,1)S(1)}, u32[]{:S(2)}, u32[]{:S(2)}) async-start(bf16[16,64,128]{2,1,0:T(8,128)(2,1)} %broadcast_in_dim.91), calls=%async_computation.6 | async-start | bytes 524288 | tf_op jit(solution)/shard_map/all_to_all | solution.py:114
  47.7 91.5 %while.36 = (s32[]{:T(128)}, bf16[16,16,128]{2,1,0:T(8,128)(2,1)S(1)}, bf16[10,16,16,128]{3,2,1,0:T(8,128)(2,1)S(1)}, pred[]{:T(512)}, s32[]{:T(128)}, /*index=5...) while((s32[]{:T(128)}, ...), condition=%wide.region_6.7_spmd.clone, body=%wide.region_5.6_spmd.clone.sunk | while | flops 98338 | bytes 3949198 | solution.py:213
  56.9 11.8 %all-to-all-done.4 = bf16[32,64,128]{2,1,0:T(8,128)(2,1)S(1)} async-done(((bf16[32,64,128]{2,1,0:T(8,128)(2,1)}), bf16[32,64,128]{2,1,0:T(8,128)(2,1)S(1)}, u32[]{:S(2)}, u32[]{:S(2)}) %all-to-all-start.4) | async-done | bytes 524320 | tf_op jit(solution)/shard_map/while/body/eval_jaxpr/all_to_all | solution.py:168
  76.3 11.8 %all-to-all-done.5 = bf16[32,64,128]{2,1,0:T(8,128)(2,1)S(1)} async-done(((bf16[32,64,128]{2,1,0:T(8,128)(2,1)}), bf16[32,64,128]{2,1,0:T(8,128)(2,1)S(1)}, u32[]{:S(2)}, u32[]{:S(2)}) %all-to-all-start.5) | async-done | bytes 524320 | tf_op jit(solution)/shard_map/while/body/eval_jaxpr/all_to_all | solution.py:168
  100.9 11.8 %all-to-all-done.4 = bf16[32,64,128]{2,1,0:T(8,128)(2,1)S(1)} async-done(((bf16[32,64,128]{2,1,0:T(8,128)(2,1)}), bf16[32,64,128]{2,1,0:T(8,128)(2,1)S(1)}, u32[]{:S(2)}, u32[]{:S(2)}) %all-to-all-start.4) | async-done | bytes 524320 | tf_op jit(solution)/shard_map/while/body/eval_jaxpr/all_to_all | solution.py:168
  120.4 11.8 %all-to-all-done.5 = bf16[32,64,128]{2,1,0:T(8,128)(2,1)S(1)} async-done(((bf16[32,64,128]{2,1,0:T(8,128)(2,1)}), bf16[32,64,128]{2,1,0:T(8,128)(2,1)S(1)}, u32[]{:S(2)}, u32[]{:S(2)}) %all-to-all-start.5) | async-done | bytes 524320 | tf_op jit(solution)/shard_map/while/body/eval_jaxpr/all_to_all | solution.py:168
  151.8 11.8 %all-to-all-done.7 = bf16[32,64,128]{2,1,0:T(8,128)(2,1)S(1)} async-done(((bf16[32,64,128]{2,1,0:T(8,128)(2,1)}), bf16[32,64,128]{2,1,0:T(8,128)(2,1)S(1)}, u32[]{:S(2)}, u32[]{:S(2)}) %all-to-all-start.7) | async-done | bytes 524320 | tf_op jit(solution)/shard_map/all_to_all | solution.py:168
  166.5 15.2 %all_to_all.135 = bf16[32,64,128]{2,1,0:T(8,128)(2,1)S(1)} all-to-all(bf16[32,64,128]{2,1,0:T(8,128)(2,1)S(1)} %bitcast.145), channel_id=1, replica_groups=mesh['section'=16,'expert'=32] {'expert'}, dimensions={0} | all-to-all | bytes 1048576 | tf_op jit(solution)/shard_map/all_to_all | solution.py:168
  189.0 11.8 %all-to-all-done.9 = bf16[32,64,128]{2,1,0:T(8,128)(2,1)S(1)} async-done(((bf16[32,64,128]{2,1,0:T(8,128)(2,1)}), bf16[32,64,128]{2,1,0:T(8,128)(2,1)S(1)}, u32[]{:S(2)}, u32[]{:S(2)}) %all-to-all-start.9) | async-done | bytes 524320 | tf_op jit(solution)/shard_map/all_to_all | solution.py:168
  203.4 15.2 %all_to_all.136 = bf16[32,64,128]{2,1,0:T(8,128)(2,1)S(1)} all-to-all(bf16[32,64,128]{2,1,0:T(8,128)(2,1)S(1)} %bitcast.155), channel_id=1, replica_groups=mesh['section'=16,'expert'=32] {'expert'}, dimensions={0} | all-to-all | bytes 1048576 | tf_op jit(solution)/shard_map/all_to_all | solution.py:168
  236.1 11.8 %all-to-all-done.11 = bf16[32,64,128]{2,1,0:T(8,128)(2,1)S(1)} async-done(((bf16[32,64,128]{2,1,0:T(8,128)(2,1)}), bf16[32,64,128]{2,1,0:T(8,128)(2,1)S(1)}, u32[]{:S(2)}, u32[]{:S(2)}) %all-to-all-start.11) | async-done | bytes 524320 | tf_op jit(solution)/shard_map/all_to_all | solution.py:168
  269.0 493.3 %while.35 = (s32[]{:T(128)}, bf16[16,16,128]{2,1,0:T(8,128)(2,1)S(1)}, bf16[10,16,16,128]{3,2,1,0:T(8,128)(2,1)S(1)}, pred[]{:T(512)}, s32[]{:T(128)}, /*index=5...) while((s32[]{:T(128)}, ...), condition=%wide.region_8.9_spmd, body=%wide.region_7.8_spmd.sunk | while | flops 65603 | bytes 6980677 | solution.py:230
  274.7 11.8 %all-to-all-done = bf16[32,64,128]{2,1,0:T(8,128)(2,1)S(1)} async-done(((bf16[32,64,128]{2,1,0:T(8,128)(2,1)}), bf16[32,64,128]{2,1,0:T(8,128)(2,1)S(1)}, u32[]{:S(2)}, u32[]{:S(2)}) %all-to-all-start) | async-done | bytes 524320 | tf_op jit(solution)/shard_map/while/body/eval_jaxpr/all_to_all | solution.py:168
  289.0 15.2 %all_to_all.137 = bf16[32,64,128]{2,1,0:T(8,128)(2,1)S(1)} all-to-all(bf16[32,64,128]{2,1,0:T(8,128)(2,1)S(1)} %bitcast.143), channel_id=1, replica_groups=mesh['section'=16,'expert'=32] {'expert'}, dimensions={0} | all-to-all | bytes 1048576 | tf_op jit(solution)/shard_map/while/body/eval_jaxpr/all_to_all | solution.py:168
  314.0 11.8 %all-to-all-done.2 = bf16[32,64,128]{2,1,0:T(8,128)(2,1)S(1)} async-done(((bf16[32,64,128]{2,1,0:T(8,128)(2,1)}), bf16[32,64,128]{2,1,0:T(8,128)(2,1)S(1)}, u32[]{:S(2)}, u32[]{:S(2)}) %all-to-all-start.2) | async-done | bytes 524320 | tf_op jit(solution)/shard_map/while/body/eval_jaxpr/all_to_all | solution.py:168
  352.6 11.8 %all-to-all-done = bf16[32,64,128]{2,1,0:T(8,128)(2,1)S(1)} async-done(((bf16[32,64,128]{2,1,0:T(8,128)(2,1)}), bf16[32,64,128]{2,1,0:T(8,128)(2,1)S(1)}, u32[]{:S(2)}, u32[]{:S(2)}) %all-to-all-start) | async-done | bytes 524320 | tf_op jit(solution)/shard_map/while/body/eval_jaxpr/all_to_all | solution.py:168
  367.0 15.2 %all_to_all.137 = bf16[32,64,128]{2,1,0:T(8,128)(2,1)S(1)} all-to-all(bf16[32,64,128]{2,1,0:T(8,128)(2,1)S(1)} %bitcast.143), channel_id=1, replica_groups=mesh['section'=16,'expert'=32] {'expert'}, dimensions={0} | all-to-all | bytes 1048576 | tf_op jit(solution)/shard_map/while/body/eval_jaxpr/all_to_all | solution.py:168
  397.2 11.8 %all-to-all-done.2 = bf16[32,64,128]{2,1,0:T(8,128)(2,1)S(1)} async-done(((bf16[32,64,128]{2,1,0:T(8,128)(2,1)}), bf16[32,64,128]{2,1,0:T(8,128)(2,1)S(1)}, u32[]{:S(2)}, u32[]{:S(2)}) %all-to-all-start.2) | async-done | bytes 524320 | tf_op jit(solution)/shard_map/while/body/eval_jaxpr/all_to_all | solution.py:168
  435.8 11.8 %all-to-all-done = bf16[32,64,128]{2,1,0:T(8,128)(2,1)S(1)} async-done(((bf16[32,64,128]{2,1,0:T(8,128)(2,1)}), bf16[32,64,128]{2,1,0:T(8,128)(2,1)S(1)}, u32[]{:S(2)}, u32[]{:S(2)}) %all-to-all-start) | async-done | bytes 524320 | tf_op jit(solution)/shard_map/while/body/eval_jaxpr/all_to_all | solution.py:168
  450.2 15.2 %all_to_all.137 = bf16[32,64,128]{2,1,0:T(8,128)(2,1)S(1)} all-to-all(bf16[32,64,128]{2,1,0:T(8,128)(2,1)S(1)} %bitcast.143), channel_id=1, replica_groups=mesh['section'=16,'expert'=32] {'expert'}, dimensions={0} | all-to-all | bytes 1048576 | tf_op jit(solution)/shard_map/while/body/eval_jaxpr/all_to_all | solution.py:168
  480.2 11.8 %all-to-all-done.2 = bf16[32,64,128]{2,1,0:T(8,128)(2,1)S(1)} async-done(((bf16[32,64,128]{2,1,0:T(8,128)(2,1)}), bf16[32,64,128]{2,1,0:T(8,128)(2,1)S(1)}, u32[]{:S(2)}, u32[]{:S(2)}) %all-to-all-start.2) | async-done | bytes 524320 | tf_op jit(solution)/shard_map/while/body/eval_jaxpr/all_to_all | solution.py:168
  518.8 11.8 %all-to-all-done = bf16[32,64,128]{2,1,0:T(8,128)(2,1)S(1)} async-done(((bf16[32,64,128]{2,1,0:T(8,128)(2,1)}), bf16[32,64,128]{2,1,0:T(8,128)(2,1)S(1)}, u32[]{:S(2)}, u32[]{:S(2)}) %all-to-all-start) | async-done | bytes 524320 | tf_op jit(solution)/shard_map/while/body/eval_jaxpr/all_to_all | solution.py:168
  533.2 15.2 %all_to_all.137 = bf16[32,64,128]{2,1,0:T(8,128)(2,1)S(1)} all-to-all(bf16[32,64,128]{2,1,0:T(8,128)(2,1)S(1)} %bitcast.143), channel_id=1, replica_groups=mesh['section'=16,'expert'=32] {'expert'}, dimensions={0} | all-to-all | bytes 1048576 | tf_op jit(solution)/shard_map/while/body/eval_jaxpr/all_to_all | solution.py:168
  563.3 11.8 %all-to-all-done.2 = bf16[32,64,128]{2,1,0:T(8,128)(2,1)S(1)} async-done(((bf16[32,64,128]{2,1,0:T(8,128)(2,1)}), bf16[32,64,128]{2,1,0:T(8,128)(2,1)S(1)}, u32[]{:S(2)}, u32[]{:S(2)}) %all-to-all-start.2) | async-done | bytes 524320 | tf_op jit(solution)/shard_map/while/body/eval_jaxpr/all_to_all | solution.py:168
  601.9 11.8 %all-to-all-done = bf16[32,64,128]{2,1,0:T(8,128)(2,1)S(1)} async-done(((bf16[32,64,128]{2,1,0:T(8,128)(2,1)}), bf16[32,64,128]{2,1,0:T(8,128)(2,1)S(1)}, u32[]{:S(2)}, u32[]{:S(2)}) %all-to-all-start) | async-done | bytes 524320 | tf_op jit(solution)/shard_map/while/body/eval_jaxpr/all_to_all | solution.py:168
  616.3 15.2 %all_to_all.137 = bf16[32,64,128]{2,1,0:T(8,128)(2,1)S(1)} all-to-all(bf16[32,64,128]{2,1,0:T(8,128)(2,1)S(1)} %bitcast.143), channel_id=1, replica_groups=mesh['section'=16,'expert'=32] {'expert'}, dimensions={0} | all-to-all | bytes 1048576 | tf_op jit(solution)/shard_map/while/body/eval_jaxpr/all_to_all | solution.py:168
  646.4 11.8 %all-to-all-done.2 = bf16[32,64,128]{2,1,0:T(8,128)(2,1)S(1)} async-done(((bf16[32,64,128]{2,1,0:T(8,128)(2,1)}), bf16[32,64,128]{2,1,0:T(8,128)(2,1)S(1)}, u32[]{:S(2)}, u32[]{:S(2)}) %all-to-all-start.2) | async-done | bytes 524320 | tf_op jit(solution)/shard_map/while/body/eval_jaxpr/all_to_all | solution.py:168
  685.0 11.8 %all-to-all-done = bf16[32,64,128]{2,1,0:T(8,128)(2,1)S(1)} async-done(((bf16[32,64,128]{2,1,0:T(8,128)(2,1)}), bf16[32,64,128]{2,1,0:T(8,128)(2,1)S(1)}, u32[]{:S(2)}, u32[]{:S(2)}) %all-to-all-start) | async-done | bytes 524320 | tf_op jit(solution)/shard_map/while/body/eval_jaxpr/all_to_all | solution.py:168
  699.3 15.2 %all_to_all.137 = bf16[32,64,128]{2,1,0:T(8,128)(2,1)S(1)} all-to-all(bf16[32,64,128]{2,1,0:T(8,128)(2,1)S(1)} %bitcast.143), channel_id=1, replica_groups=mesh['section'=16,'expert'=32] {'expert'}, dimensions={0} | all-to-all | bytes 1048576 | tf_op jit(solution)/shard_map/while/body/eval_jaxpr/all_to_all | solution.py:168
  729.4 11.8 %all-to-all-done.2 = bf16[32,64,128]{2,1,0:T(8,128)(2,1)S(1)} async-done(((bf16[32,64,128]{2,1,0:T(8,128)(2,1)}), bf16[32,64,128]{2,1,0:T(8,128)(2,1)S(1)}, u32[]{:S(2)}, u32[]{:S(2)}) %all-to-all-start.2) | async-done | bytes 524320 | tf_op jit(solution)/shard_map/while/body/eval_jaxpr/all_to_all | solution.py:168
  767.9 11.8 %all-to-all-done.13 = bf16[32,64,128]{2,1,0:T(8,128)(2,1)S(1)} async-done(((bf16[32,64,128]{2,1,0:T(8,128)(2,1)}), bf16[32,64,128]{2,1,0:T(8,128)(2,1)S(1)}, u32[]{:S(2)}, u32[]{:S(2)}) %all-to-all-start.13) | async-done | bytes 524320 | tf_op jit(solution)/shard_map/all_to_all | solution.py:168
  805.3 11.8 %all-to-all-done.15 = bf16[32,64,128]{2,1,0:T(8,128)(2,1)S(1)} async-done(((bf16[32,64,128]{2,1,0:T(8,128)(2,1)}), bf16[32,64,128]{2,1,0:T(8,128)(2,1)S(1)}, u32[]{:S(2)}, u32[]{:S(2)}) %all-to-all-start.15) | async-done | bytes 524320 | tf_op jit(solution)/shard_map/all_to_all | solution.py:168
  (227 shorter events, 464.6 us)
Async XLA Ops:
  5.6 32.9 %all-to-all-start.6 = ((bf16[16,64,128]{2,1,0:T(8,128)(2,1)}), bf16[16,64,128]{2,1,0:T(8,128)(2,1)S(1)}, u32[]{:S(2)}, u32[]{:S(2)}) async-start(bf16[16,64,128]{2,1,0:T(8,128)(2,1)} %broadcast_in_dim.91), calls=%async_computation.6 | async-start | bytes 524288 | tf_op jit(solution)/shard_map/all_to_all | solution.py:114
  38.7 100.5 %collective-permute-start.4 = (bf16[2048,384]{1,0:T(8,128)(2,1)}, bf16[2048,384]{1,0:T(8,128)(2,1)S(1)}, u32[]{:S(2)}, u32[]{:S(2)}) collective-permute-start(bf16[2048,384]{1,0:T(8,128)(2,1)} %bitcast.26.refs_0_), channel_id=1, source_target_pairs={{64,96},{96,64},{128,160},{160,128},{192,224},{224,192},{256,288},... | collective-permute-start | bytes 4718600 | tf_op jit(solution)/shard_map/ppermute | solution.py:132
  41.7 97.6 %collective-permute-start.5 = (bf16[2048,384]{1,0:T(8,128)(2,1)}, bf16[2048,384]{1,0:T(8,128)(2,1)}, u32[]{:S(2)}, u32[]{:S(2)}) collective-permute-start(bf16[2048,384]{1,0:T(8,128)(2,1)} %bitcast.27.refs_1_), channel_id=1, source_target_pairs={{64,96},{96,64},{128,160},{160,128},{192,224},{224,192},{256,288},... | collective-permute-start | bytes 4718600 | tf_op jit(solution)/shard_map/ppermute | solution.py:132
  44.6 98.1 %collective-permute-start.6 = (bf16[384,2048]{1,0:T(8,128)(2,1)}, bf16[384,2048]{1,0:T(8,128)(2,1)}, u32[]{:S(2)}, u32[]{:S(2)}) collective-permute-start(bf16[384,2048]{1,0:T(8,128)(2,1)} %bitcast.28.refs_2_), channel_id=1, source_target_pairs={{64,96},{96,64},{128,160},{160,128},{192,224},{224,192},{256,288},... | collective-permute-start | bytes 4718600 | tf_op jit(solution)/shard_map/ppermute | solution.py:132
  49.5 19.1 %all-to-all-start.4 = ((bf16[32,64,128]{2,1,0:T(8,128)(2,1)}), bf16[32,64,128]{2,1,0:T(8,128)(2,1)S(1)}, u32[]{:S(2)}, u32[]{:S(2)}) async-start(bf16[32,64,128]{2,1,0:T(8,128)(2,1)} %bitcast.133), calls=%async_computation.4 | async-start | bytes 1048576 | tf_op jit(solution)/shard_map/while/body/eval_jaxpr/all_to_all | solution.py:168
  72.4 15.7 %all-to-all-start.5 = ((bf16[32,64,128]{2,1,0:T(8,128)(2,1)}), bf16[32,64,128]{2,1,0:T(8,128)(2,1)S(1)}, u32[]{:S(2)}, u32[]{:S(2)}) async-start(bf16[32,64,128]{2,1,0:T(8,128)(2,1)} %bitcast.135), calls=%async_computation.5 | async-start | bytes 1048576 | tf_op jit(solution)/shard_map/while/body/eval_jaxpr/all_to_all | solution.py:168
  97.0 15.7 %all-to-all-start.4 = ((bf16[32,64,128]{2,1,0:T(8,128)(2,1)}), bf16[32,64,128]{2,1,0:T(8,128)(2,1)S(1)}, u32[]{:S(2)}, u32[]{:S(2)}) async-start(bf16[32,64,128]{2,1,0:T(8,128)(2,1)} %bitcast.133), calls=%async_computation.4 | async-start | bytes 1048576 | tf_op jit(solution)/shard_map/while/body/eval_jaxpr/all_to_all | solution.py:168
  116.4 15.7 %all-to-all-start.5 = ((bf16[32,64,128]{2,1,0:T(8,128)(2,1)}), bf16[32,64,128]{2,1,0:T(8,128)(2,1)S(1)}, u32[]{:S(2)}, u32[]{:S(2)}) async-start(bf16[32,64,128]{2,1,0:T(8,128)(2,1)} %bitcast.135), calls=%async_computation.5 | async-start | bytes 1048576 | tf_op jit(solution)/shard_map/while/body/eval_jaxpr/all_to_all | solution.py:168
  144.4 19.1 %all-to-all-start.7 = ((bf16[32,64,128]{2,1,0:T(8,128)(2,1)}), bf16[32,64,128]{2,1,0:T(8,128)(2,1)S(1)}, u32[]{:S(2)}, u32[]{:S(2)}) async-start(bf16[32,64,128]{2,1,0:T(8,128)(2,1)} %bitcast.37), calls=%async_computation.7 | async-start | bytes 1048576 | tf_op jit(solution)/shard_map/all_to_all | solution.py:168
  185.1 15.7 %all-to-all-start.9 = ((bf16[32,64,128]{2,1,0:T(8,128)(2,1)}), bf16[32,64,128]{2,1,0:T(8,128)(2,1)S(1)}, u32[]{:S(2)}, u32[]{:S(2)}) async-start(bf16[32,64,128]{2,1,0:T(8,128)(2,1)} %bitcast.41), calls=%async_computation.9 | async-start | bytes 1048576 | tf_op jit(solution)/shard_map/all_to_all | solution.py:168
  232.2 15.7 %all-to-all-start.11 = ((bf16[32,64,128]{2,1,0:T(8,128)(2,1)}), bf16[32,64,128]{2,1,0:T(8,128)(2,1)S(1)}, u32[]{:S(2)}, u32[]{:S(2)}) async-start(bf16[32,64,128]{2,1,0:T(8,128)(2,1)} %bitcast.45), calls=%async_computation.11 | async-start | bytes 1048576 | tf_op jit(solution)/shard_map/all_to_all | solution.py:168
  251.6 15.7 %all-to-all-start.12 = ((bf16[32,64,128]{2,1,0:T(8,128)(2,1)}), bf16[32,64,128]{2,1,0:T(8,128)(2,1)S(1)}, u32[]{:S(2)}, u32[]{:S(2)}) async-start(bf16[32,64,128]{2,1,0:T(8,128)(2,1)} %bitcast.47), calls=%async_computation.12 | async-start | bytes 1048576 | tf_op jit(solution)/shard_map/all_to_all | solution.py:168
  270.8 15.7 %all-to-all-start = ((bf16[32,64,128]{2,1,0:T(8,128)(2,1)}), bf16[32,64,128]{2,1,0:T(8,128)(2,1)S(1)}, u32[]{:S(2)}, u32[]{:S(2)}) async-start(bf16[32,64,128]{2,1,0:T(8,128)(2,1)} %bitcast.121), calls=%async_computation | async-start | bytes 1048576 | tf_op jit(solution)/shard_map/while/body/eval_jaxpr/all_to_all | solution.py:168
  310.1 15.7 %all-to-all-start.2 = ((bf16[32,64,128]{2,1,0:T(8,128)(2,1)}), bf16[32,64,128]{2,1,0:T(8,128)(2,1)S(1)}, u32[]{:S(2)}, u32[]{:S(2)}) async-start(bf16[32,64,128]{2,1,0:T(8,128)(2,1)} %bitcast.125), calls=%async_computation.2 | async-start | bytes 1048576 | tf_op jit(solution)/shard_map/while/body/eval_jaxpr/all_to_all | solution.py:168
  329.6 15.7 %all-to-all-start.3 = ((bf16[32,64,128]{2,1,0:T(8,128)(2,1)}), bf16[32,64,128]{2,1,0:T(8,128)(2,1)S(1)}, u32[]{:S(2)}, u32[]{:S(2)}) async-start(bf16[32,64,128]{2,1,0:T(8,128)(2,1)} %bitcast.127), calls=%async_computation.3 | async-start | bytes 1048576 | tf_op jit(solution)/shard_map/while/body/eval_jaxpr/all_to_all | solution.py:168
  348.7 15.7 %all-to-all-start = ((bf16[32,64,128]{2,1,0:T(8,128)(2,1)}), bf16[32,64,128]{2,1,0:T(8,128)(2,1)S(1)}, u32[]{:S(2)}, u32[]{:S(2)}) async-start(bf16[32,64,128]{2,1,0:T(8,128)(2,1)} %bitcast.121), calls=%async_computation | async-start | bytes 1048576 | tf_op jit(solution)/shard_map/while/body/eval_jaxpr/all_to_all | solution.py:168
  393.3 15.7 %all-to-all-start.2 = ((bf16[32,64,128]{2,1,0:T(8,128)(2,1)}), bf16[32,64,128]{2,1,0:T(8,128)(2,1)S(1)}, u32[]{:S(2)}, u32[]{:S(2)}) async-start(bf16[32,64,128]{2,1,0:T(8,128)(2,1)} %bitcast.125), calls=%async_computation.2 | async-start | bytes 1048576 | tf_op jit(solution)/shard_map/while/body/eval_jaxpr/all_to_all | solution.py:168
  412.7 15.7 %all-to-all-start.3 = ((bf16[32,64,128]{2,1,0:T(8,128)(2,1)}), bf16[32,64,128]{2,1,0:T(8,128)(2,1)S(1)}, u32[]{:S(2)}, u32[]{:S(2)}) async-start(bf16[32,64,128]{2,1,0:T(8,128)(2,1)} %bitcast.127), calls=%async_computation.3 | async-start | bytes 1048576 | tf_op jit(solution)/shard_map/while/body/eval_jaxpr/all_to_all | solution.py:168
  431.9 15.7 %all-to-all-start = ((bf16[32,64,128]{2,1,0:T(8,128)(2,1)}), bf16[32,64,128]{2,1,0:T(8,128)(2,1)S(1)}, u32[]{:S(2)}, u32[]{:S(2)}) async-start(bf16[32,64,128]{2,1,0:T(8,128)(2,1)} %bitcast.121), calls=%async_computation | async-start | bytes 1048576 | tf_op jit(solution)/shard_map/while/body/eval_jaxpr/all_to_all | solution.py:168
  476.3 15.7 %all-to-all-start.2 = ((bf16[32,64,128]{2,1,0:T(8,128)(2,1)}), bf16[32,64,128]{2,1,0:T(8,128)(2,1)S(1)}, u32[]{:S(2)}, u32[]{:S(2)}) async-start(bf16[32,64,128]{2,1,0:T(8,128)(2,1)} %bitcast.125), calls=%async_computation.2 | async-start | bytes 1048576 | tf_op jit(solution)/shard_map/while/body/eval_jaxpr/all_to_all | solution.py:168
  495.8 15.7 %all-to-all-start.3 = ((bf16[32,64,128]{2,1,0:T(8,128)(2,1)}), bf16[32,64,128]{2,1,0:T(8,128)(2,1)S(1)}, u32[]{:S(2)}, u32[]{:S(2)}) async-start(bf16[32,64,128]{2,1,0:T(8,128)(2,1)} %bitcast.127), calls=%async_computation.3 | async-start | bytes 1048576 | tf_op jit(solution)/shard_map/while/body/eval_jaxpr/all_to_all | solution.py:168
  559.4 15.7 %all-to-all-start.2 = ((bf16[32,64,128]{2,1,0:T(8,128)(2,1)}), bf16[32,64,128]{2,1,0:T(8,128)(2,1)S(1)}, u32[]{:S(2)}, u32[]{:S(2)}) async-start(bf16[32,64,128]{2,1,0:T(8,128)(2,1)} %bitcast.125), calls=%async_computation.2 | async-start | bytes 1048576 | tf_op jit(solution)/shard_map/while/body/eval_jaxpr/all_to_all | solution.py:168
  578.8 15.7 %all-to-all-start.3 = ((bf16[32,64,128]{2,1,0:T(8,128)(2,1)}), bf16[32,64,128]{2,1,0:T(8,128)(2,1)S(1)}, u32[]{:S(2)}, u32[]{:S(2)}) async-start(bf16[32,64,128]{2,1,0:T(8,128)(2,1)} %bitcast.127), calls=%async_computation.3 | async-start | bytes 1048576 | tf_op jit(solution)/shard_map/while/body/eval_jaxpr/all_to_all | solution.py:168
  598.0 15.7 %all-to-all-start = ((bf16[32,64,128]{2,1,0:T(8,128)(2,1)}), bf16[32,64,128]{2,1,0:T(8,128)(2,1)S(1)}, u32[]{:S(2)}, u32[]{:S(2)}) async-start(bf16[32,64,128]{2,1,0:T(8,128)(2,1)} %bitcast.121), calls=%async_computation | async-start | bytes 1048576 | tf_op jit(solution)/shard_map/while/body/eval_jaxpr/all_to_all | solution.py:168
  642.4 15.7 %all-to-all-start.2 = ((bf16[32,64,128]{2,1,0:T(8,128)(2,1)}), bf16[32,64,128]{2,1,0:T(8,128)(2,1)S(1)}, u32[]{:S(2)}, u32[]{:S(2)}) async-start(bf16[32,64,128]{2,1,0:T(8,128)(2,1)} %bitcast.125), calls=%async_computation.2 | async-start | bytes 1048576 | tf_op jit(solution)/shard_map/while/body/eval_jaxpr/all_to_all | solution.py:168
  661.9 15.7 %all-to-all-start.3 = ((bf16[32,64,128]{2,1,0:T(8,128)(2,1)}), bf16[32,64,128]{2,1,0:T(8,128)(2,1)S(1)}, u32[]{:S(2)}, u32[]{:S(2)}) async-start(bf16[32,64,128]{2,1,0:T(8,128)(2,1)} %bitcast.127), calls=%async_computation.3 | async-start | bytes 1048576 | tf_op jit(solution)/shard_map/while/body/eval_jaxpr/all_to_all | solution.py:168
  681.1 15.7 %all-to-all-start = ((bf16[32,64,128]{2,1,0:T(8,128)(2,1)}), bf16[32,64,128]{2,1,0:T(8,128)(2,1)S(1)}, u32[]{:S(2)}, u32[]{:S(2)}) async-start(bf16[32,64,128]{2,1,0:T(8,128)(2,1)} %bitcast.121), calls=%async_computation | async-start | bytes 1048576 | tf_op jit(solution)/shard_map/while/body/eval_jaxpr/all_to_all | solution.py:168
  725.5 15.7 %all-to-all-start.2 = ((bf16[32,64,128]{2,1,0:T(8,128)(2,1)}), bf16[32,64,128]{2,1,0:T(8,128)(2,1)S(1)}, u32[]{:S(2)}, u32[]{:S(2)}) async-start(bf16[32,64,128]{2,1,0:T(8,128)(2,1)} %bitcast.125), calls=%async_computation.2 | async-start | bytes 1048576 | tf_op jit(solution)/shard_map/while/body/eval_jaxpr/all_to_all | solution.py:168
  744.9 15.7 %all-to-all-start.3 = ((bf16[32,64,128]{2,1,0:T(8,128)(2,1)}), bf16[32,64,128]{2,1,0:T(8,128)(2,1)S(1)}, u32[]{:S(2)}, u32[]{:S(2)}) async-start(bf16[32,64,128]{2,1,0:T(8,128)(2,1)} %bitcast.127), calls=%async_computation.3 | async-start | bytes 1048576 | tf_op jit(solution)/shard_map/while/body/eval_jaxpr/all_to_all | solution.py:168
  764.0 15.7 %all-to-all-start.13 = ((bf16[32,64,128]{2,1,0:T(8,128)(2,1)}), bf16[32,64,128]{2,1,0:T(8,128)(2,1)S(1)}, u32[]{:S(2)}, u32[]{:S(2)}) async-start(bf16[32,64,128]{2,1,0:T(8,128)(2,1)} %bitcast.54), calls=%async_computation.13 | async-start | bytes 1048576 | tf_op jit(solution)/shard_map/all_to_all | solution.py:168
  783.1 15.7 %all-to-all-start.14 = ((bf16[32,64,128]{2,1,0:T(8,128)(2,1)}), bf16[32,64,128]{2,1,0:T(8,128)(2,1)S(1)}, u32[]{:S(2)}, u32[]{:S(2)}) async-start(bf16[32,64,128]{2,1,0:T(8,128)(2,1)} %bitcast.56), calls=%async_computation.14 | async-start | bytes 1048576 | tf_op jit(solution)/shard_map/all_to_all | solution.py:168
  820.9 15.7 %all-to-all-start.16 = ((bf16[32,64,128]{2,1,0:T(8,128)(2,1)}), bf16[32,64,128]{2,1,0:T(8,128)(2,1)S(1)}, u32[]{:S(2)}, u32[]{:S(2)}) async-start(bf16[32,64,128]{2,1,0:T(8,128)(2,1)} %bitcast.63), calls=%async_computation.16 | async-start | bytes 1048576 | tf_op jit(solution)/shard_map/all_to_all | solution.py:168
  (21 other events, 124.3 us)

commit v4 on v3

--- a/solution.py
+++ b/solution.py
@@ -168,6 +168,7 @@
     exchange = lambda a: lax.all_to_all(a, "expert", split_axis=0, concat_axis=0, tiled=True)
 
     def layer(turn, held, hidden, weights):
+        turn, held, hidden = lax.optimization_barrier((jnp.int32(turn), held, hidden))
         second = jnp.where(stage == 0, column, (turn - column) % 2)
         group = turn - 2 * stage - second
         active = (group >= 0) & (group < groups)
@@ -175,10 +176,14 @@
         own = ((stage == 0) | (second == column)).astype(jnp.int32).reshape(1)
         at = pick.reshape(1)
         gain_now = lax.dynamic_slice_in_dim(gains, second * parts, parts, 0)
+        at, pick, own, gain_now, held, hidden = lax.optimization_barrier(
+            (at, pick, own, gain_now, held, hidden)
+        )
         sent = place(at, source, held, gain_now)
         arrived = exchange(sent.reshape(experts, slots * parts, lanes))
         results = expert(own, arrived.reshape(experts * slots, parts, lanes), *weights)
         returned = exchange(results.reshape(experts, slots * parts, lanes))
+        returned, pick = lax.optimization_barrier((returned, pick))
         output = mix(at, slot, share, returned.reshape(experts * slots, parts, lanes), held)
         return output, lax.dynamic_update_index_in_dim(hidden, output, pick, 0)
 
@@ -221,8 +226,9 @@
 
     def advance(i, state):
         held, hidden = state
-        for step in range(2):
-            turn = groups + 1 + 2 * i + step
+        start = groups + 1 + 2 * i
+        turns = lax.optimization_barrier((start, start + 1))
+        for step, turn in enumerate(turns):
             held, hidden = layer(turn, held, hidden, all_weights)
             held = move(held, steady_pairs((groups + 2 + step) % 2))
         return held, hidden

time: 856 us -> 835 us (0.975)
  blocking collectives: 122 us -> 418 us
  waiting for transfers between devices: 398 us -> 179 us
  starting transfers between devices: 204 us -> 123 us
  Pallas kernels: 113 us -> 97.8 us
    all_to_all x8 -> x27, blocking collectives: 122 us -> 418 us  [local(): lax.all_to_all(a, 'expert', split_axis=0, concat_axis=0, tiled=True)]
    all_to_all x30 -> x11, waiting for transfers between devices: 352 us -> 129 us  [local(): lax.all_to_all(a, 'expert', split_axis=0, concat_axis=0, tiled=True)]
    all_to_all x30 -> x11, starting transfers between devices: 124 us -> 42.9 us  [local(): lax.all_to_all(a, 'expert', split_axis=0, concat_axis=0, tiled=True)]
    pallas_call x19, Pallas kernels: 32.3 us -> 17.1 us  [layer(): sent = place(at, source, held, gain_now)]
  transfers between devices with their start and end apart: 53 -> 34, of which waited for: 43 -> 24; matrix products, arithmetic and copies ran while one was open for 0% -> 0% of each run, Pallas kernels for 2% -> 1%
where the time goes in v4:
time: 835 us; the launch traced here: 832 us
  blocking collectives  418 us (50%)
  waiting for transfers between devices  179 us (21%)
  starting transfers between devices  123 us (15%)
  Pallas kernels  97.8 us (12%)
    all_to_all x27, blocking collectives, local(): lax.all_to_all(a, 'expert', split_axis=0, concat_axis=0, tiled=True)  418 us
    all_to_all x11, waiting for transfers between devices, local(): lax.all_to_all(a, 'expert', split_axis=0, concat_axis=0, tiled=True)  129 us
    pallas_call x19, Pallas kernels, expert(): pl.pallas_call(expert_kernel, out_shape=bf(experts * slots, parts, lanes)...  62.3 us
    ppermute x17, starting transfers between devices, move(): return jnp.where(here, lax.ppermute(value, 'section', pairs), value)  45.3 us
    all_to_all x11, starting transfers between devices, local(): lax.all_to_all(a, 'expert', split_axis=0, concat_axis=0, tiled=True)  42.9 us
    ppermute x17, waiting for transfers between devices, move(): return jnp.where(here, lax.ppermute(value, 'section', pairs), value)  27.7 us
    pallas_call x19, Pallas kernels, layer(): mix(at, slot, share, returned.reshape(experts * slots, parts, lanes), held)  18.5 us
    pallas_call x19, Pallas kernels, layer(): sent = place(at, source, held, gain_now)  17.1 us
  transfers between devices with their start and end apart: 34, of which 24 were waited for; matrix products, arithmetic and copies ran while one was open for 0% of the time, Pallas kernels for 1%

profile of v4, /device:TPU:64, one launch (start us, length us, event | category | flops | bytes accessed | tf_op | source)
XLA Modules:
  0.0 831.9 jit_solution(1400014682625793309)
XLA Ops:
  7.4 14.8 %all-to-all-start.6 = ((bf16[16,64,128]{2,1,0:T(8,128)(2,1)}), bf16[16,64,128]{2,1,0:T(8,128)(2,1)S(1)}, u32[]{:S(2)}, u32[]{:S(2)}) async-start(bf16[16,64,128]{2,1,0:T(8,128)(2,1)} %broadcast_in_dim.87), calls=%async_computation.6 | async-start | bytes 524288 | tf_op jit(solution)/shard_map/all_to_all | solution.py:114
  49.4 89.3 %while.36 = (s32[]{:T(128)}, bf16[16,16,128]{2,1,0:T(8,128)(2,1)S(1)}, bf16[10,16,16,128]{3,2,1,0:T(8,128)(2,1)S(1)}, pred[]{:T(512)}, pred[]{:T(512)}, /*index=...) while((s32[]{:T(128)}, ...), condition=%wide.region_6.7_spmd.clone, body=%wide.region_5.6_spmd.clone.sunk | while | flops 98338 | bytes 3424878 | solution.py:218
  50.4 18.9 %all_to_all.145 = bf16[32,64,128]{2,1,0:T(8,128)(2,1)S(1)} all-to-all(bf16[32,64,128]{2,1,0:T(8,128)(2,1)S(1)} %bitcast.141), channel_id=1, replica_groups=mesh['section'=16,'expert'=32] {'expert'}, dimensions={0} | all-to-all | bytes 1048576 | tf_op jit(solution)/shard_map/while/body/eval_jaxpr/all_to_all | solution.py:168
  77.0 11.8 %all-to-all-done.5 = bf16[32,64,128]{2,1,0:T(8,128)(2,1)S(1)} async-done(((bf16[32,64,128]{2,1,0:T(8,128)(2,1)}), bf16[32,64,128]{2,1,0:T(8,128)(2,1)S(1)}, u32[]{:S(2)}, u32[]{:S(2)}) %all-to-all-start.5) | async-done | bytes 524320 | tf_op jit(solution)/shard_map/while/body/eval_jaxpr/all_to_all | solution.py:168
  96.9 15.2 %all_to_all.145 = bf16[32,64,128]{2,1,0:T(8,128)(2,1)S(1)} all-to-all(bf16[32,64,128]{2,1,0:T(8,128)(2,1)S(1)} %bitcast.141), channel_id=1, replica_groups=mesh['section'=16,'expert'=32] {'expert'}, dimensions={0} | all-to-all | bytes 1048576 | tf_op jit(solution)/shard_map/while/body/eval_jaxpr/all_to_all | solution.py:168
  145.4 18.9 %all_to_all.135 = bf16[32,64,128]{2,1,0:T(8,128)(2,1)S(1)} all-to-all(bf16[32,64,128]{2,1,0:T(8,128)(2,1)S(1)} %bitcast.154), channel_id=1, replica_groups=mesh['section'=16,'expert'=32] {'expert'}, dimensions={0} | all-to-all | bytes 1048576 | tf_op jit(solution)/shard_map/all_to_all | solution.py:168
  186.4 15.2 %all_to_all.136 = bf16[32,64,128]{2,1,0:T(8,128)(2,1)S(1)} all-to-all(bf16[32,64,128]{2,1,0:T(8,128)(2,1)S(1)} %bitcast.155), channel_id=1, replica_groups=mesh['section'=16,'expert'=32] {'expert'}, dimensions={0} | all-to-all | bytes 1048576 | tf_op jit(solution)/shard_map/all_to_all | solution.py:168
  233.5 15.1 %all_to_all.137 = bf16[32,64,128]{2,1,0:T(8,128)(2,1)S(1)} all-to-all(bf16[32,64,128]{2,1,0:T(8,128)(2,1)S(1)} %bitcast.156), channel_id=1, replica_groups=mesh['section'=16,'expert'=32] {'expert'}, dimensions={0} | all-to-all | bytes 1048576 | tf_op jit(solution)/shard_map/all_to_all | solution.py:168
  270.0 478.9 %while.35 = (s32[]{:T(128)}, bf16[16,16,128]{2,1,0:T(8,128)(2,1)S(1)}, bf16[10,16,16,128]{3,2,1,0:T(8,128)(2,1)S(1)}, pred[]{:T(512)}, pred[]{:T(512)}, /*index=...) while((s32[]{:T(128)}, ...), condition=%wide.region_8.9_spmd, body=%wide.region_7.8_spmd.sunk | while | flops 65603 | bytes 5932037 | solution.py:236
  271.0 15.2 %all_to_all.142 = bf16[32,64,128]{2,1,0:T(8,128)(2,1)S(1)} all-to-all(bf16[32,64,128]{2,1,0:T(8,128)(2,1)S(1)} %bitcast.142), channel_id=1, replica_groups=mesh['section'=16,'expert'=32] {'expert'}, dimensions={0} | all-to-all | bytes 1048576 | tf_op jit(solution)/shard_map/while/body/eval_jaxpr/all_to_all | solution.py:168
  288.8 15.2 %all_to_all.143 = bf16[32,64,128]{2,1,0:T(8,128)(2,1)S(1)} all-to-all(bf16[32,64,128]{2,1,0:T(8,128)(2,1)S(1)} %bitcast.145), channel_id=1, replica_groups=mesh['section'=16,'expert'=32] {'expert'}, dimensions={0} | all-to-all | bytes 1048576 | tf_op jit(solution)/shard_map/while/body/eval_jaxpr/all_to_all | solution.py:168
  309.3 15.2 %all_to_all.144 = bf16[32,64,128]{2,1,0:T(8,128)(2,1)S(1)} all-to-all(bf16[32,64,128]{2,1,0:T(8,128)(2,1)S(1)} %bitcast.143), channel_id=1, replica_groups=mesh['section'=16,'expert'=32] {'expert'}, dimensions={0} | all-to-all | bytes 1048576 | tf_op jit(solution)/shard_map/while/body/eval_jaxpr/all_to_all | solution.py:168
  346.7 15.2 %all_to_all.142 = bf16[32,64,128]{2,1,0:T(8,128)(2,1)S(1)} all-to-all(bf16[32,64,128]{2,1,0:T(8,128)(2,1)S(1)} %bitcast.142), channel_id=1, replica_groups=mesh['section'=16,'expert'=32] {'expert'}, dimensions={0} | all-to-all | bytes 1048576 | tf_op jit(solution)/shard_map/while/body/eval_jaxpr/all_to_all | solution.py:168
  364.5 15.2 %all_to_all.143 = bf16[32,64,128]{2,1,0:T(8,128)(2,1)S(1)} all-to-all(bf16[32,64,128]{2,1,0:T(8,128)(2,1)S(1)} %bitcast.145), channel_id=1, replica_groups=mesh['section'=16,'expert'=32] {'expert'}, dimensions={0} | all-to-all | bytes 1048576 | tf_op jit(solution)/shard_map/while/body/eval_jaxpr/all_to_all | solution.py:168
  390.0 15.2 %all_to_all.144 = bf16[32,64,128]{2,1,0:T(8,128)(2,1)S(1)} all-to-all(bf16[32,64,128]{2,1,0:T(8,128)(2,1)S(1)} %bitcast.143), channel_id=1, replica_groups=mesh['section'=16,'expert'=32] {'expert'}, dimensions={0} | all-to-all | bytes 1048576 | tf_op jit(solution)/shard_map/while/body/eval_jaxpr/all_to_all | solution.py:168
  412.9 11.8 %all-to-all-done.3 = bf16[32,64,128]{2,1,0:T(8,128)(2,1)S(1)} async-done(((bf16[32,64,128]{2,1,0:T(8,128)(2,1)}), bf16[32,64,128]{2,1,0:T(8,128)(2,1)S(1)}, u32[]{:S(2)}, u32[]{:S(2)}) %all-to-all-start.3) | async-done | bytes 524320 | tf_op jit(solution)/shard_map/while/body/eval_jaxpr/all_to_all | solution.py:168
  427.3 15.2 %all_to_all.142 = bf16[32,64,128]{2,1,0:T(8,128)(2,1)S(1)} all-to-all(bf16[32,64,128]{2,1,0:T(8,128)(2,1)S(1)} %bitcast.142), channel_id=1, replica_groups=mesh['section'=16,'expert'=32] {'expert'}, dimensions={0} | all-to-all | bytes 1048576 | tf_op jit(solution)/shard_map/while/body/eval_jaxpr/all_to_all | solution.py:168
  445.2 15.2 %all_to_all.143 = bf16[32,64,128]{2,1,0:T(8,128)(2,1)S(1)} all-to-all(bf16[32,64,128]{2,1,0:T(8,128)(2,1)S(1)} %bitcast.145), channel_id=1, replica_groups=mesh['section'=16,'expert'=32] {'expert'}, dimensions={0} | all-to-all | bytes 1048576 | tf_op jit(solution)/shard_map/while/body/eval_jaxpr/all_to_all | solution.py:168
  470.6 15.2 %all_to_all.144 = bf16[32,64,128]{2,1,0:T(8,128)(2,1)S(1)} all-to-all(bf16[32,64,128]{2,1,0:T(8,128)(2,1)S(1)} %bitcast.143), channel_id=1, replica_groups=mesh['section'=16,'expert'=32] {'expert'}, dimensions={0} | all-to-all | bytes 1048576 | tf_op jit(solution)/shard_map/while/body/eval_jaxpr/all_to_all | solution.py:168
  508.0 15.2 %all_to_all.142 = bf16[32,64,128]{2,1,0:T(8,128)(2,1)S(1)} all-to-all(bf16[32,64,128]{2,1,0:T(8,128)(2,1)S(1)} %bitcast.142), channel_id=1, replica_groups=mesh['section'=16,'expert'=32] {'expert'}, dimensions={0} | all-to-all | bytes 1048576 | tf_op jit(solution)/shard_map/while/body/eval_jaxpr/all_to_all | solution.py:168
  525.8 15.2 %all_to_all.143 = bf16[32,64,128]{2,1,0:T(8,128)(2,1)S(1)} all-to-all(bf16[32,64,128]{2,1,0:T(8,128)(2,1)S(1)} %bitcast.145), channel_id=1, replica_groups=mesh['section'=16,'expert'=32] {'expert'}, dimensions={0} | all-to-all | bytes 1048576 | tf_op jit(solution)/shard_map/while/body/eval_jaxpr/all_to_all | solution.py:168
  551.2 15.2 %all_to_all.144 = bf16[32,64,128]{2,1,0:T(8,128)(2,1)S(1)} all-to-all(bf16[32,64,128]{2,1,0:T(8,128)(2,1)S(1)} %bitcast.143), channel_id=1, replica_groups=mesh['section'=16,'expert'=32] {'expert'}, dimensions={0} | all-to-all | bytes 1048576 | tf_op jit(solution)/shard_map/while/body/eval_jaxpr/all_to_all | solution.py:168
  588.6 15.2 %all_to_all.142 = bf16[32,64,128]{2,1,0:T(8,128)(2,1)S(1)} all-to-all(bf16[32,64,128]{2,1,0:T(8,128)(2,1)S(1)} %bitcast.142), channel_id=1, replica_groups=mesh['section'=16,'expert'=32] {'expert'}, dimensions={0} | all-to-all | bytes 1048576 | tf_op jit(solution)/shard_map/while/body/eval_jaxpr/all_to_all | solution.py:168
  606.4 15.2 %all_to_all.143 = bf16[32,64,128]{2,1,0:T(8,128)(2,1)S(1)} all-to-all(bf16[32,64,128]{2,1,0:T(8,128)(2,1)S(1)} %bitcast.145), channel_id=1, replica_groups=mesh['section'=16,'expert'=32] {'expert'}, dimensions={0} | all-to-all | bytes 1048576 | tf_op jit(solution)/shard_map/while/body/eval_jaxpr/all_to_all | solution.py:168
  631.9 15.2 %all_to_all.144 = bf16[32,64,128]{2,1,0:T(8,128)(2,1)S(1)} all-to-all(bf16[32,64,128]{2,1,0:T(8,128)(2,1)S(1)} %bitcast.143), channel_id=1, replica_groups=mesh['section'=16,'expert'=32] {'expert'}, dimensions={0} | all-to-all | bytes 1048576 | tf_op jit(solution)/shard_map/while/body/eval_jaxpr/all_to_all | solution.py:168
  669.2 15.2 %all_to_all.142 = bf16[32,64,128]{2,1,0:T(8,128)(2,1)S(1)} all-to-all(bf16[32,64,128]{2,1,0:T(8,128)(2,1)S(1)} %bitcast.142), channel_id=1, replica_groups=mesh['section'=16,'expert'=32] {'expert'}, dimensions={0} | all-to-all | bytes 1048576 | tf_op jit(solution)/shard_map/while/body/eval_jaxpr/all_to_all | solution.py:168
  687.1 15.2 %all_to_all.143 = bf16[32,64,128]{2,1,0:T(8,128)(2,1)S(1)} all-to-all(bf16[32,64,128]{2,1,0:T(8,128)(2,1)S(1)} %bitcast.145), channel_id=1, replica_groups=mesh['section'=16,'expert'=32] {'expert'}, dimensions={0} | all-to-all | bytes 1048576 | tf_op jit(solution)/shard_map/while/body/eval_jaxpr/all_to_all | solution.py:168
  712.5 15.2 %all_to_all.144 = bf16[32,64,128]{2,1,0:T(8,128)(2,1)S(1)} all-to-all(bf16[32,64,128]{2,1,0:T(8,128)(2,1)S(1)} %bitcast.143), channel_id=1, replica_groups=mesh['section'=16,'expert'=32] {'expert'}, dimensions={0} | all-to-all | bytes 1048576 | tf_op jit(solution)/shard_map/while/body/eval_jaxpr/all_to_all | solution.py:168
  749.9 15.2 %all_to_all.138 = bf16[32,64,128]{2,1,0:T(8,128)(2,1)S(1)} all-to-all(bf16[32,64,128]{2,1,0:T(8,128)(2,1)S(1)} %bitcast.157), channel_id=1, replica_groups=mesh['section'=16,'expert'=32] {'expert'}, dimensions={0} | all-to-all | bytes 1048576 | tf_op jit(solution)/shard_map/all_to_all | solution.py:168
  767.7 15.2 %all_to_all.139 = bf16[32,64,128]{2,1,0:T(8,128)(2,1)S(1)} all-to-all(bf16[32,64,128]{2,1,0:T(8,128)(2,1)S(1)} %bitcast.163), channel_id=1, replica_groups=mesh['section'=16,'expert'=32] {'expert'}, dimensions={0} | all-to-all | bytes 1048576 | tf_op jit(solution)/shard_map/all_to_all | solution.py:168
  784.9 15.2 %all_to_all.140 = bf16[32,64,128]{2,1,0:T(8,128)(2,1)S(1)} all-to-all(bf16[32,64,128]{2,1,0:T(8,128)(2,1)S(1)} %bitcast.153), channel_id=1, replica_groups=mesh['section'=16,'expert'=32] {'expert'}, dimensions={0} | all-to-all | bytes 1048576 | tf_op jit(solution)/shard_map/all_to_all | solution.py:168
  803.1 15.2 %all_to_all.141 = bf16[32,64,128]{2,1,0:T(8,128)(2,1)S(1)} all-to-all(bf16[32,64,128]{2,1,0:T(8,128)(2,1)S(1)} %bitcast.159), channel_id=1, replica_groups=mesh['section'=16,'expert'=32] {'expert'}, dimensions={0} | all-to-all | bytes 1048576 | tf_op jit(solution)/shard_map/all_to_all | solution.py:168
  (218 shorter events, 372.9 us)
Async XLA Ops:
  7.4 32.9 %all-to-all-start.6 = ((bf16[16,64,128]{2,1,0:T(8,128)(2,1)}), bf16[16,64,128]{2,1,0:T(8,128)(2,1)S(1)}, u32[]{:S(2)}, u32[]{:S(2)}) async-start(bf16[16,64,128]{2,1,0:T(8,128)(2,1)} %broadcast_in_dim.87), calls=%async_computation.6 | async-start | bytes 524288 | tf_op jit(solution)/shard_map/all_to_all | solution.py:114
  23.2 9.4 %collective-permute-start.3 = (f32[31,128]{1,0:T(8,128)S(1)}, f32[31,128]{1,0:T(8,128)S(1)}, u32[]{:S(2)}, u32[]{:S(2)}) collective-permute-start(f32[31,128]{1,0:T(8,128)S(1)} %fusion.2), channel_id=1, source_target_pairs={{0,32},{32,0},{64,96},{96,64},{128,160},{160,128},{192,224},{224,1... | collective-permute-start | bytes 47624 | tf_op jit(solution)/shard_map/ppermute | solution.py:121
  40.5 98.3 %collective-permute-start.4 = (bf16[2048,384]{1,0:T(8,128)(2,1)}, bf16[2048,384]{1,0:T(8,128)(2,1)S(1)}, u32[]{:S(2)}, u32[]{:S(2)}) collective-permute-start(bf16[2048,384]{1,0:T(8,128)(2,1)} %bitcast.14.refs_0_), channel_id=1, source_target_pairs={{64,96},{96,64},{128,160},{160,128},{192,224},{224,192},{256,288},... | collective-permute-start | bytes 4718600 | tf_op jit(solution)/shard_map/ppermute | solution.py:132
  43.4 95.3 %collective-permute-start.5 = (bf16[2048,384]{1,0:T(8,128)(2,1)}, bf16[2048,384]{1,0:T(8,128)(2,1)}, u32[]{:S(2)}, u32[]{:S(2)}) collective-permute-start(bf16[2048,384]{1,0:T(8,128)(2,1)} %bitcast.15.refs_1_), channel_id=1, source_target_pairs={{64,96},{96,64},{128,160},{160,128},{192,224},{224,192},{256,288},... | collective-permute-start | bytes 4718600 | tf_op jit(solution)/shard_map/ppermute | solution.py:132
  46.3 98.1 %collective-permute-start.6 = (bf16[384,2048]{1,0:T(8,128)(2,1)}, bf16[384,2048]{1,0:T(8,128)(2,1)}, u32[]{:S(2)}, u32[]{:S(2)}) collective-permute-start(bf16[384,2048]{1,0:T(8,128)(2,1)} %bitcast.16.refs_2_), channel_id=1, source_target_pairs={{64,96},{96,64},{128,160},{160,128},{192,224},{224,192},{256,288},... | collective-permute-start | bytes 4718600 | tf_op jit(solution)/shard_map/ppermute | solution.py:132
  73.1 15.7 %all-to-all-start.5 = ((bf16[32,64,128]{2,1,0:T(8,128)(2,1)}), bf16[32,64,128]{2,1,0:T(8,128)(2,1)S(1)}, u32[]{:S(2)}, u32[]{:S(2)}) async-start(bf16[32,64,128]{2,1,0:T(8,128)(2,1)} %bitcast.135), calls=%async_computation.5 | async-start | bytes 1048576 | tf_op jit(solution)/shard_map/while/body/eval_jaxpr/all_to_all | solution.py:168
  89.7 6.2 collective-permute-start.2
  115.9 15.7 %all-to-all-start.5 = ((bf16[32,64,128]{2,1,0:T(8,128)(2,1)}), bf16[32,64,128]{2,1,0:T(8,128)(2,1)S(1)}, u32[]{:S(2)}, u32[]{:S(2)}) async-start(bf16[32,64,128]{2,1,0:T(8,128)(2,1)} %bitcast.135), calls=%async_computation.5 | async-start | bytes 1048576 | tf_op jit(solution)/shard_map/while/body/eval_jaxpr/all_to_all | solution.py:168
  132.5 6.2 collective-permute-start.2
  168.0 15.7 %all-to-all-start.8 = ((bf16[32,64,128]{2,1,0:T(8,128)(2,1)}), bf16[32,64,128]{2,1,0:T(8,128)(2,1)S(1)}, u32[]{:S(2)}, u32[]{:S(2)}) async-start(bf16[32,64,128]{2,1,0:T(8,128)(2,1)} %bitcast.35), calls=%async_computation.8 | async-start | bytes 1048576 | tf_op jit(solution)/shard_map/all_to_all | solution.py:168
  184.7 0.7 collective-permute-start.7
  205.0 15.7 %all-to-all-start.10 = ((bf16[32,64,128]{2,1,0:T(8,128)(2,1)}), bf16[32,64,128]{2,1,0:T(8,128)(2,1)S(1)}, u32[]{:S(2)}, u32[]{:S(2)}) async-start(bf16[32,64,128]{2,1,0:T(8,128)(2,1)} %bitcast.42), calls=%async_computation.10 | async-start | bytes 1048576 | tf_op jit(solution)/shard_map/all_to_all | solution.py:168
  221.7 10.9 %collective-permute-start.8 = (bf16[16,16,128]{2,1,0:T(8,128)(2,1)S(1)}, bf16[16,16,128]{2,1,0:T(8,128)(2,1)S(1)}, u32[]{:S(2)}, u32[]{:S(2)}) collective-permute-start(bf16[16,16,128]{2,1,0:T(8,128)(2,1)S(1)} %mix.30), channel_id=1, source_target_pairs={{0,32},{32,64},{64,128},{1,33},{33,65},{65,129},{2,34},{34,66},{66... | collective-permute-start | bytes 196616 | tf_op jit(solution)/shard_map/ppermute | solution.py:192
  252.4 15.7 %all-to-all-start.12 = ((bf16[32,64,128]{2,1,0:T(8,128)(2,1)}), bf16[32,64,128]{2,1,0:T(8,128)(2,1)S(1)}, u32[]{:S(2)}, u32[]{:S(2)}) async-start(bf16[32,64,128]{2,1,0:T(8,128)(2,1)} %bitcast.49), calls=%async_computation.12 | async-start | bytes 1048576 | tf_op jit(solution)/shard_map/all_to_all | solution.py:168
  269.1 0.9 collective-permute-start.9
  305.0 3.3 collective-permute-start
  328.3 15.7 %all-to-all-start.3 = ((bf16[32,64,128]{2,1,0:T(8,128)(2,1)}), bf16[32,64,128]{2,1,0:T(8,128)(2,1)S(1)}, u32[]{:S(2)}, u32[]{:S(2)}) async-start(bf16[32,64,128]{2,1,0:T(8,128)(2,1)} %bitcast.127), calls=%async_computation.3 | async-start | bytes 1048576 | tf_op jit(solution)/shard_map/while/body/eval_jaxpr/all_to_all | solution.py:168
  345.0 0.7 collective-permute-start.1
  380.7 8.3 collective-permute-start
  409.0 15.7 %all-to-all-start.3 = ((bf16[32,64,128]{2,1,0:T(8,128)(2,1)}), bf16[32,64,128]{2,1,0:T(8,128)(2,1)S(1)}, u32[]{:S(2)}, u32[]{:S(2)}) async-start(bf16[32,64,128]{2,1,0:T(8,128)(2,1)} %bitcast.127), calls=%async_computation.3 | async-start | bytes 1048576 | tf_op jit(solution)/shard_map/while/body/eval_jaxpr/all_to_all | solution.py:168
  461.3 8.3 collective-permute-start
  489.6 15.7 %all-to-all-start.3 = ((bf16[32,64,128]{2,1,0:T(8,128)(2,1)}), bf16[32,64,128]{2,1,0:T(8,128)(2,1)S(1)}, u32[]{:S(2)}, u32[]{:S(2)}) async-start(bf16[32,64,128]{2,1,0:T(8,128)(2,1)} %bitcast.127), calls=%async_computation.3 | async-start | bytes 1048576 | tf_op jit(solution)/shard_map/while/body/eval_jaxpr/all_to_all | solution.py:168
  506.2 0.7 collective-permute-start.1
  542.0 8.3 collective-permute-start
  570.2 15.7 %all-to-all-start.3 = ((bf16[32,64,128]{2,1,0:T(8,128)(2,1)}), bf16[32,64,128]{2,1,0:T(8,128)(2,1)S(1)}, u32[]{:S(2)}, u32[]{:S(2)}) async-start(bf16[32,64,128]{2,1,0:T(8,128)(2,1)} %bitcast.127), calls=%async_computation.3 | async-start | bytes 1048576 | tf_op jit(solution)/shard_map/while/body/eval_jaxpr/all_to_all | solution.py:168
  586.9 0.7 collective-permute-start.1
  622.6 8.3 collective-permute-start
  650.9 15.7 %all-to-all-start.3 = ((bf16[32,64,128]{2,1,0:T(8,128)(2,1)}), bf16[32,64,128]{2,1,0:T(8,128)(2,1)S(1)}, u32[]{:S(2)}, u32[]{:S(2)}) async-start(bf16[32,64,128]{2,1,0:T(8,128)(2,1)} %bitcast.127), calls=%async_computation.3 | async-start | bytes 1048576 | tf_op jit(solution)/shard_map/while/body/eval_jaxpr/all_to_all | solution.py:168
  667.5 0.7 collective-permute-start.1
  703.3 8.3 collective-permute-start
  731.5 15.7 %all-to-all-start.3 = ((bf16[32,64,128]{2,1,0:T(8,128)(2,1)}), bf16[32,64,128]{2,1,0:T(8,128)(2,1)S(1)}, u32[]{:S(2)}, u32[]{:S(2)}) async-start(bf16[32,64,128]{2,1,0:T(8,128)(2,1)} %bitcast.127), calls=%async_computation.3 | async-start | bytes 1048576 | tf_op jit(solution)/shard_map/while/body/eval_jaxpr/all_to_all | solution.py:168
  819.4 11.6 %collective-permute-start.10 = (bf16[2,16,16,128]{3,2,1,0:T(8,128)(2,1)S(1)}, bf16[2,16,16,128]{3,2,1,0:T(8,128)(2,1)S(1)}, u32[]{:S(2)}, u32[]{:S(2)}) collective-permute-start(bf16[2,16,16,128]{3,2,1,0:T(8,128)(2,1)S(1)} %slice_select_fusion), channel_id=1, source_target_pairs={{0,32},{32,0},{64,96},{96,64},{128,160},{160,128},{192,224},{224,1... | collective-permute-start | bytes 393224 | tf_op jit(solution)/shard_map/ppermute | solution.py:242
  (2 other events, 1.4 us)

commit v5 on v4

--- a/solution.py
+++ b/solution.py
@@ -188,7 +188,8 @@
         return output, lax.dynamic_update_index_in_dim(hidden, output, pick, 0)
 
     def move(value, pairs):
-        here = functools.reduce(jnp.logical_or, [section == b for _, b in pairs])
+        value, at = lax.optimization_barrier((value, section))
+        here = functools.reduce(jnp.logical_or, [at == b for _, b in pairs])
         return jnp.where(here, lax.ppermute(value, "section", pairs), value)
 
     def opening_pairs(turn):
@@ -234,12 +235,12 @@
         return held, hidden
 
     held, hidden = lax.fori_loop(0, (last - 2 - groups) // 2, advance, (held, hidden))
-    for turn in (last - 1, last):
-        held, hidden = layer(turn, held, hidden, all_weights)
-
+    held, hidden = layer(last - 1, held, hidden, all_weights)
     low, high = hidden[:groups], hidden[groups + 1 : 2 * groups + 1]
     theirs = jnp.where(column == 0, high[0::2], low[1::2])
     theirs = lax.ppermute(theirs, "section", swap)
+    _, hidden = layer(last, held, hidden, all_weights)
+    low, high = hidden[:groups], hidden[groups + 1 : 2 * groups + 1]
     mine = jnp.where(column == 0, low, high)
     result = [
         jnp.where((stage == 0) | (column == j % 2), mine[j], theirs[j // 2]) for j in range(groups)

time: 835 us -> 825 us (0.988)
  the two profiles are of different devices: /device:TPU:64 before, /device:TPU:97 now
where the time goes in v5:
time: 825 us; the launch traced here: 822 us
  blocking collectives  445 us (54%)
  waiting for transfers between devices  160 us (19%)
  starting transfers between devices  106 us (13%)
  Pallas kernels  97.1 us (12%)
    all_to_all x28, blocking collectives, local(): lax.all_to_all(a, 'expert', split_axis=0, concat_axis=0, tiled=True)  445 us
    all_to_all x10, waiting for transfers between devices, local(): lax.all_to_all(a, 'expert', split_axis=0, concat_axis=0, tiled=True)  115 us
    pallas_call x19, Pallas kernels, expert(): pl.pallas_call(expert_kernel, out_shape=bf(experts * slots, parts, lanes)...  61.6 us
    ppermute x17, starting transfers between devices, move(): return jnp.where(here, lax.ppermute(value, 'section', pairs), value)  41 us
    all_to_all x10, starting transfers between devices, local(): lax.all_to_all(a, 'expert', split_axis=0, concat_axis=0, tiled=True)  40 us
    ppermute x17, waiting for transfers between devices, move(): return jnp.where(here, lax.ppermute(value, 'section', pairs), value)  18.8 us
    pallas_call x19, Pallas kernels, layer(): mix(at, slot, share, returned.reshape(experts * slots, parts, lanes), held)  18.5 us
    pallas_call x19, Pallas kernels, layer(): sent = place(at, source, held, gain_now)  17.1 us
  transfers between devices with their start and end apart: 33, of which 21 were waited for; matrix products, arithmetic and copies ran while one was open for 1% of the time, Pallas kernels for 1%

profile of v5, /device:TPU:97, one launch (start us, length us, event | category | flops | bytes accessed | tf_op | source)
XLA Modules:
  0.0 822.0 jit_solution(6316867586648296670)
XLA Ops:
  5.6 13.7 %all-to-all-start.6 = ((bf16[16,64,128]{2,1,0:T(8,128)(2,1)}), bf16[16,64,128]{2,1,0:T(8,128)(2,1)S(1)}, u32[]{:S(2)}, u32[]{:S(2)}) async-start(bf16[16,64,128]{2,1,0:T(8,128)(2,1)} %broadcast_in_dim.87), calls=%async_computation.6 | async-start | bytes 524288 | tf_op jit(solution)/shard_map/all_to_all | solution.py:114
  44.1 81.3 %while.36 = (s32[]{:T(128)}, bf16[16,16,128]{2,1,0:T(8,128)(2,1)S(1)}, bf16[10,16,16,128]{3,2,1,0:T(8,128)(2,1)S(1)}, pred[]{:T(512)}, bf16[4,16,16,128]{3,2,1,0...) while((s32[]{:T(128)}, ...), condition=%wide.region_6.7_spmd.clone, body=%wide.region_5.6_spmd.clone.sunk | while | flops 98341 | bytes 3424899 | solution.py:219
  45.1 21.7 %all_to_all.146 = bf16[32,64,128]{2,1,0:T(8,128)(2,1)S(1)} all-to-all(bf16[32,64,128]{2,1,0:T(8,128)(2,1)S(1)} %bitcast.141), channel_id=1, replica_groups=mesh['section'=16,'expert'=32] {'expert'}, dimensions={0} | all-to-all | bytes 1048576 | tf_op jit(solution)/shard_map/while/body/eval_jaxpr/all_to_all | solution.py:168
  89.0 15.2 %all_to_all.146 = bf16[32,64,128]{2,1,0:T(8,128)(2,1)S(1)} all-to-all(bf16[32,64,128]{2,1,0:T(8,128)(2,1)S(1)} %bitcast.141), channel_id=1, replica_groups=mesh['section'=16,'expert'=32] {'expert'}, dimensions={0} | all-to-all | bytes 1048576 | tf_op jit(solution)/shard_map/while/body/eval_jaxpr/all_to_all | solution.py:168
  125.5 15.0 %collective-permute-done.6.refs_5_ = bf16[384,2048]{1,0:T(8,128)(2,1)} collective-permute-done((bf16[384,2048]{1,0:T(8,128)(2,1)}, bf16[384,2048]{1,0:T(8,128)(2,1)}, u32[]{:S(2)}, u32[]{:S(2)}) %collective-permute-start.6) | collective-permute-done | bytes 1572896 | tf_op jit(solution)/shard_map/ppermute | solution.py:132
  141.5 21.1 %all_to_all.135 = bf16[32,64,128]{2,1,0:T(8,128)(2,1)S(1)} all-to-all(bf16[32,64,128]{2,1,0:T(8,128)(2,1)S(1)} %bitcast.155), channel_id=1, replica_groups=mesh['section'=16,'expert'=32] {'expert'}, dimensions={0} | all-to-all | bytes 1048576 | tf_op jit(solution)/shard_map/all_to_all | solution.py:168
  165.6 15.2 %all_to_all.136 = bf16[32,64,128]{2,1,0:T(8,128)(2,1)S(1)} all-to-all(bf16[32,64,128]{2,1,0:T(8,128)(2,1)S(1)} %bitcast.148), channel_id=1, replica_groups=mesh['section'=16,'expert'=32] {'expert'}, dimensions={0} | all-to-all | bytes 1048576 | tf_op jit(solution)/shard_map/all_to_all | solution.py:168
  188.7 16.4 %all_to_all.137 = bf16[32,64,128]{2,1,0:T(8,128)(2,1)S(1)} all-to-all(bf16[32,64,128]{2,1,0:T(8,128)(2,1)S(1)} %bitcast.156), channel_id=1, replica_groups=mesh['section'=16,'expert'=32] {'expert'}, dimensions={0} | all-to-all | bytes 1048576 | tf_op jit(solution)/shard_map/all_to_all | solution.py:168
  207.7 15.2 %all_to_all.138 = bf16[32,64,128]{2,1,0:T(8,128)(2,1)S(1)} all-to-all(bf16[32,64,128]{2,1,0:T(8,128)(2,1)S(1)} %bitcast.161), channel_id=1, replica_groups=mesh['section'=16,'expert'=32] {'expert'}, dimensions={0} | all-to-all | bytes 1048576 | tf_op jit(solution)/shard_map/all_to_all | solution.py:168
  225.6 15.2 %all_to_all.139 = bf16[32,64,128]{2,1,0:T(8,128)(2,1)S(1)} all-to-all(bf16[32,64,128]{2,1,0:T(8,128)(2,1)S(1)} %bitcast.157), channel_id=1, replica_groups=mesh['section'=16,'expert'=32] {'expert'}, dimensions={0} | all-to-all | bytes 1048576 | tf_op jit(solution)/shard_map/all_to_all | solution.py:168
  269.8 478.7 %while.35 = (s32[]{:T(128)}, bf16[16,16,128]{2,1,0:T(8,128)(2,1)S(1)}, bf16[10,16,16,128]{3,2,1,0:T(8,128)(2,1)S(1)}, s32[]{:T(128)}, s32[]{:T(128)}, /*index=5*...) while((s32[]{:T(128)}, ...), condition=%wide.region_8.9_spmd, body=%wide.region_7.8_spmd.sunk | while | flops 65625 | bytes 5932231 | solution.py:237
  270.8 15.7 %all_to_all.143 = bf16[32,64,128]{2,1,0:T(8,128)(2,1)S(1)} all-to-all(bf16[32,64,128]{2,1,0:T(8,128)(2,1)S(1)} %bitcast.142), channel_id=1, replica_groups=mesh['section'=16,'expert'=32] {'expert'}, dimensions={0} | all-to-all | bytes 1048576 | tf_op jit(solution)/shard_map/while/body/eval_jaxpr/all_to_all | solution.py:168
  289.1 15.2 %all_to_all.144 = bf16[32,64,128]{2,1,0:T(8,128)(2,1)S(1)} all-to-all(bf16[32,64,128]{2,1,0:T(8,128)(2,1)S(1)} %bitcast.145), channel_id=1, replica_groups=mesh['section'=16,'expert'=32] {'expert'}, dimensions={0} | all-to-all | bytes 1048576 | tf_op jit(solution)/shard_map/while/body/eval_jaxpr/all_to_all | solution.py:168
  307.0 15.2 %all_to_all.145 = bf16[32,64,128]{2,1,0:T(8,128)(2,1)S(1)} all-to-all(bf16[32,64,128]{2,1,0:T(8,128)(2,1)S(1)} %bitcast.143), channel_id=1, replica_groups=mesh['section'=16,'expert'=32] {'expert'}, dimensions={0} | all-to-all | bytes 1048576 | tf_op jit(solution)/shard_map/while/body/eval_jaxpr/all_to_all | solution.py:168
  346.3 15.8 %all_to_all.143 = bf16[32,64,128]{2,1,0:T(8,128)(2,1)S(1)} all-to-all(bf16[32,64,128]{2,1,0:T(8,128)(2,1)S(1)} %bitcast.142), channel_id=1, replica_groups=mesh['section'=16,'expert'=32] {'expert'}, dimensions={0} | all-to-all | bytes 1048576 | tf_op jit(solution)/shard_map/while/body/eval_jaxpr/all_to_all | solution.py:168
  364.7 15.2 %all_to_all.144 = bf16[32,64,128]{2,1,0:T(8,128)(2,1)S(1)} all-to-all(bf16[32,64,128]{2,1,0:T(8,128)(2,1)S(1)} %bitcast.145), channel_id=1, replica_groups=mesh['section'=16,'expert'=32] {'expert'}, dimensions={0} | all-to-all | bytes 1048576 | tf_op jit(solution)/shard_map/while/body/eval_jaxpr/all_to_all | solution.py:168
  382.6 15.2 %all_to_all.145 = bf16[32,64,128]{2,1,0:T(8,128)(2,1)S(1)} all-to-all(bf16[32,64,128]{2,1,0:T(8,128)(2,1)S(1)} %bitcast.143), channel_id=1, replica_groups=mesh['section'=16,'expert'=32] {'expert'}, dimensions={0} | all-to-all | bytes 1048576 | tf_op jit(solution)/shard_map/while/body/eval_jaxpr/all_to_all | solution.py:168
  426.7 16.1 %all_to_all.143 = bf16[32,64,128]{2,1,0:T(8,128)(2,1)S(1)} all-to-all(bf16[32,64,128]{2,1,0:T(8,128)(2,1)S(1)} %bitcast.142), channel_id=1, replica_groups=mesh['section'=16,'expert'=32] {'expert'}, dimensions={0} | all-to-all | bytes 1048576 | tf_op jit(solution)/shard_map/while/body/eval_jaxpr/all_to_all | solution.py:168
  445.4 15.2 %all_to_all.144 = bf16[32,64,128]{2,1,0:T(8,128)(2,1)S(1)} all-to-all(bf16[32,64,128]{2,1,0:T(8,128)(2,1)S(1)} %bitcast.145), channel_id=1, replica_groups=mesh['section'=16,'expert'=32] {'expert'}, dimensions={0} | all-to-all | bytes 1048576 | tf_op jit(solution)/shard_map/while/body/eval_jaxpr/all_to_all | solution.py:168
  463.3 15.2 %all_to_all.145 = bf16[32,64,128]{2,1,0:T(8,128)(2,1)S(1)} all-to-all(bf16[32,64,128]{2,1,0:T(8,128)(2,1)S(1)} %bitcast.143), channel_id=1, replica_groups=mesh['section'=16,'expert'=32] {'expert'}, dimensions={0} | all-to-all | bytes 1048576 | tf_op jit(solution)/shard_map/while/body/eval_jaxpr/all_to_all | solution.py:168
  507.4 16.1 %all_to_all.143 = bf16[32,64,128]{2,1,0:T(8,128)(2,1)S(1)} all-to-all(bf16[32,64,128]{2,1,0:T(8,128)(2,1)S(1)} %bitcast.142), channel_id=1, replica_groups=mesh['section'=16,'expert'=32] {'expert'}, dimensions={0} | all-to-all | bytes 1048576 | tf_op jit(solution)/shard_map/while/body/eval_jaxpr/all_to_all | solution.py:168
  526.1 15.2 %all_to_all.144 = bf16[32,64,128]{2,1,0:T(8,128)(2,1)S(1)} all-to-all(bf16[32,64,128]{2,1,0:T(8,128)(2,1)S(1)} %bitcast.145), channel_id=1, replica_groups=mesh['section'=16,'expert'=32] {'expert'}, dimensions={0} | all-to-all | bytes 1048576 | tf_op jit(solution)/shard_map/while/body/eval_jaxpr/all_to_all | solution.py:168
  544.0 15.2 %all_to_all.145 = bf16[32,64,128]{2,1,0:T(8,128)(2,1)S(1)} all-to-all(bf16[32,64,128]{2,1,0:T(8,128)(2,1)S(1)} %bitcast.143), channel_id=1, replica_groups=mesh['section'=16,'expert'=32] {'expert'}, dimensions={0} | all-to-all | bytes 1048576 | tf_op jit(solution)/shard_map/while/body/eval_jaxpr/all_to_all | solution.py:168
  588.1 16.1 %all_to_all.143 = bf16[32,64,128]{2,1,0:T(8,128)(2,1)S(1)} all-to-all(bf16[32,64,128]{2,1,0:T(8,128)(2,1)S(1)} %bitcast.142), channel_id=1, replica_groups=mesh['section'=16,'expert'=32] {'expert'}, dimensions={0} | all-to-all | bytes 1048576 | tf_op jit(solution)/shard_map/while/body/eval_jaxpr/all_to_all | solution.py:168
  606.8 15.2 %all_to_all.144 = bf16[32,64,128]{2,1,0:T(8,128)(2,1)S(1)} all-to-all(bf16[32,64,128]{2,1,0:T(8,128)(2,1)S(1)} %bitcast.145), channel_id=1, replica_groups=mesh['section'=16,'expert'=32] {'expert'}, dimensions={0} | all-to-all | bytes 1048576 | tf_op jit(solution)/shard_map/while/body/eval_jaxpr/all_to_all | solution.py:168
  624.7 15.2 %all_to_all.145 = bf16[32,64,128]{2,1,0:T(8,128)(2,1)S(1)} all-to-all(bf16[32,64,128]{2,1,0:T(8,128)(2,1)S(1)} %bitcast.143), channel_id=1, replica_groups=mesh['section'=16,'expert'=32] {'expert'}, dimensions={0} | all-to-all | bytes 1048576 | tf_op jit(solution)/shard_map/while/body/eval_jaxpr/all_to_all | solution.py:168
  668.8 16.1 %all_to_all.143 = bf16[32,64,128]{2,1,0:T(8,128)(2,1)S(1)} all-to-all(bf16[32,64,128]{2,1,0:T(8,128)(2,1)S(1)} %bitcast.142), channel_id=1, replica_groups=mesh['section'=16,'expert'=32] {'expert'}, dimensions={0} | all-to-all | bytes 1048576 | tf_op jit(solution)/shard_map/while/body/eval_jaxpr/all_to_all | solution.py:168
  687.5 15.2 %all_to_all.144 = bf16[32,64,128]{2,1,0:T(8,128)(2,1)S(1)} all-to-all(bf16[32,64,128]{2,1,0:T(8,128)(2,1)S(1)} %bitcast.145), channel_id=1, replica_groups=mesh['section'=16,'expert'=32] {'expert'}, dimensions={0} | all-to-all | bytes 1048576 | tf_op jit(solution)/shard_map/while/body/eval_jaxpr/all_to_all | solution.py:168
  705.4 15.2 %all_to_all.145 = bf16[32,64,128]{2,1,0:T(8,128)(2,1)S(1)} all-to-all(bf16[32,64,128]{2,1,0:T(8,128)(2,1)S(1)} %bitcast.143), channel_id=1, replica_groups=mesh['section'=16,'expert'=32] {'expert'}, dimensions={0} | all-to-all | bytes 1048576 | tf_op jit(solution)/shard_map/while/body/eval_jaxpr/all_to_all | solution.py:168
  749.5 16.1 %all_to_all.140 = bf16[32,64,128]{2,1,0:T(8,128)(2,1)S(1)} all-to-all(bf16[32,64,128]{2,1,0:T(8,128)(2,1)S(1)} %bitcast.158), channel_id=1, replica_groups=mesh['section'=16,'expert'=32] {'expert'}, dimensions={0} | all-to-all | bytes 1048576 | tf_op jit(solution)/shard_map/all_to_all | solution.py:168
  768.2 15.2 %all_to_all.141 = bf16[32,64,128]{2,1,0:T(8,128)(2,1)S(1)} all-to-all(bf16[32,64,128]{2,1,0:T(8,128)(2,1)S(1)} %bitcast.164), channel_id=1, replica_groups=mesh['section'=16,'expert'=32] {'expert'}, dimensions={0} | all-to-all | bytes 1048576 | tf_op jit(solution)/shard_map/all_to_all | solution.py:168
  785.4 15.2 %all_to_all.142 = bf16[32,64,128]{2,1,0:T(8,128)(2,1)S(1)} all-to-all(bf16[32,64,128]{2,1,0:T(8,128)(2,1)S(1)} %bitcast.154), channel_id=1, replica_groups=mesh['section'=16,'expert'=32] {'expert'}, dimensions={0} | all-to-all | bytes 1048576 | tf_op jit(solution)/shard_map/all_to_all | solution.py:168
  (218 shorter events, 345.3 us)
Async XLA Ops:
  5.6 31.0 %all-to-all-start.6 = ((bf16[16,64,128]{2,1,0:T(8,128)(2,1)}), bf16[16,64,128]{2,1,0:T(8,128)(2,1)S(1)}, u32[]{:S(2)}, u32[]{:S(2)}) async-start(bf16[16,64,128]{2,1,0:T(8,128)(2,1)} %broadcast_in_dim.87), calls=%async_computation.6 | async-start | bytes 524288 | tf_op jit(solution)/shard_map/all_to_all | solution.py:114
  22.2 9.4 %collective-permute-start.3 = (f32[31,128]{1,0:T(8,128)S(1)}, f32[31,128]{1,0:T(8,128)S(1)}, u32[]{:S(2)}, u32[]{:S(2)}) collective-permute-start(f32[31,128]{1,0:T(8,128)S(1)} %fusion.2), channel_id=1, source_target_pairs={{0,32},{32,0},{64,96},{96,64},{128,160},{160,128},{192,224},{224,1... | collective-permute-start | bytes 47624 | tf_op jit(solution)/shard_map/ppermute | solution.py:121
  36.8 88.7 %collective-permute-start.4 = (bf16[2048,384]{1,0:T(8,128)(2,1)}, bf16[2048,384]{1,0:T(8,128)(2,1)S(1)}, u32[]{:S(2)}, u32[]{:S(2)}) collective-permute-start(bf16[2048,384]{1,0:T(8,128)(2,1)} %bitcast.14.refs_0_), channel_id=1, source_target_pairs={{64,96},{96,64},{128,160},{160,128},{192,224},{224,192},{256,288},... | collective-permute-start | bytes 4718600 | tf_op jit(solution)/shard_map/ppermute | solution.py:132
  38.7 86.8 %collective-permute-start.5 = (bf16[2048,384]{1,0:T(8,128)(2,1)}, bf16[2048,384]{1,0:T(8,128)(2,1)}, u32[]{:S(2)}, u32[]{:S(2)}) collective-permute-start(bf16[2048,384]{1,0:T(8,128)(2,1)} %bitcast.15.refs_1_), channel_id=1, source_target_pairs={{64,96},{96,64},{128,160},{160,128},{192,224},{224,192},{256,288},... | collective-permute-start | bytes 4718600 | tf_op jit(solution)/shard_map/ppermute | solution.py:132
  42.1 98.4 %collective-permute-start.6 = (bf16[384,2048]{1,0:T(8,128)(2,1)}, bf16[384,2048]{1,0:T(8,128)(2,1)}, u32[]{:S(2)}, u32[]{:S(2)}) collective-permute-start(bf16[384,2048]{1,0:T(8,128)(2,1)} %bitcast.16.refs_2_), channel_id=1, source_target_pairs={{64,96},{96,64},{128,160},{160,128},{192,224},{224,192},{256,288},... | collective-permute-start | bytes 4718600 | tf_op jit(solution)/shard_map/ppermute | solution.py:132
  70.6 15.7 %all-to-all-start.5 = ((bf16[32,64,128]{2,1,0:T(8,128)(2,1)}), bf16[32,64,128]{2,1,0:T(8,128)(2,1)S(1)}, u32[]{:S(2)}, u32[]{:S(2)}) async-start(bf16[32,64,128]{2,1,0:T(8,128)(2,1)} %bitcast.135), calls=%async_computation.5 | async-start | bytes 1048576 | tf_op jit(solution)/shard_map/while/body/eval_jaxpr/all_to_all | solution.py:168
  87.3 0.7 collective-permute-start.2
  108.0 15.7 %all-to-all-start.5 = ((bf16[32,64,128]{2,1,0:T(8,128)(2,1)}), bf16[32,64,128]{2,1,0:T(8,128)(2,1)S(1)}, u32[]{:S(2)}, u32[]{:S(2)}) async-start(bf16[32,64,128]{2,1,0:T(8,128)(2,1)} %bitcast.135), calls=%async_computation.5 | async-start | bytes 1048576 | tf_op jit(solution)/shard_map/while/body/eval_jaxpr/all_to_all | solution.py:168
  181.8 5.9 collective-permute-start.7
  223.9 0.7 collective-permute-start.8
  244.6 15.7 %all-to-all-start.12 = ((bf16[32,64,128]{2,1,0:T(8,128)(2,1)}), bf16[32,64,128]{2,1,0:T(8,128)(2,1)S(1)}, u32[]{:S(2)}, u32[]{:S(2)}) async-start(bf16[32,64,128]{2,1,0:T(8,128)(2,1)} %bitcast.49), calls=%async_computation.12 | async-start | bytes 1048576 | tf_op jit(solution)/shard_map/all_to_all | solution.py:168
  261.3 8.5 %collective-permute-start.9 = (bf16[16,16,128]{2,1,0:T(8,128)(2,1)S(1)}, bf16[16,16,128]{2,1,0:T(8,128)(2,1)S(1)}, u32[]{:S(2)}, u32[]{:S(2)}) collective-permute-start(bf16[16,16,128]{2,1,0:T(8,128)(2,1)S(1)} %mix.31), channel_id=1, source_target_pairs={{32,96},{96,160},{33,97},{97,161},{34,98},{98,162},{35,99},{99,163... | collective-permute-start | bytes 196616 | tf_op jit(solution)/shard_map/ppermute | solution.py:193
  305.3 0.7 collective-permute-start
  326.0 15.7 %all-to-all-start.3 = ((bf16[32,64,128]{2,1,0:T(8,128)(2,1)}), bf16[32,64,128]{2,1,0:T(8,128)(2,1)S(1)}, u32[]{:S(2)}, u32[]{:S(2)}) async-start(bf16[32,64,128]{2,1,0:T(8,128)(2,1)} %bitcast.127), calls=%async_computation.3 | async-start | bytes 1048576 | tf_op jit(solution)/shard_map/while/body/eval_jaxpr/all_to_all | solution.py:168
  342.7 2.6 collective-permute-start.1
  380.9 0.7 collective-permute-start
  401.6 15.7 %all-to-all-start.3 = ((bf16[32,64,128]{2,1,0:T(8,128)(2,1)}), bf16[32,64,128]{2,1,0:T(8,128)(2,1)S(1)}, u32[]{:S(2)}, u32[]{:S(2)}) async-start(bf16[32,64,128]{2,1,0:T(8,128)(2,1)} %bitcast.127), calls=%async_computation.3 | async-start | bytes 1048576 | tf_op jit(solution)/shard_map/while/body/eval_jaxpr/all_to_all | solution.py:168
  418.3 7.4 collective-permute-start.1
  461.6 0.7 collective-permute-start
  482.3 15.7 %all-to-all-start.3 = ((bf16[32,64,128]{2,1,0:T(8,128)(2,1)}), bf16[32,64,128]{2,1,0:T(8,128)(2,1)S(1)}, u32[]{:S(2)}, u32[]{:S(2)}) async-start(bf16[32,64,128]{2,1,0:T(8,128)(2,1)} %bitcast.127), calls=%async_computation.3 | async-start | bytes 1048576 | tf_op jit(solution)/shard_map/while/body/eval_jaxpr/all_to_all | solution.py:168
  499.0 7.4 collective-permute-start.1
  542.3 0.7 collective-permute-start
  563.0 15.7 %all-to-all-start.3 = ((bf16[32,64,128]{2,1,0:T(8,128)(2,1)}), bf16[32,64,128]{2,1,0:T(8,128)(2,1)S(1)}, u32[]{:S(2)}, u32[]{:S(2)}) async-start(bf16[32,64,128]{2,1,0:T(8,128)(2,1)} %bitcast.127), calls=%async_computation.3 | async-start | bytes 1048576 | tf_op jit(solution)/shard_map/while/body/eval_jaxpr/all_to_all | solution.py:168
  579.7 7.4 collective-permute-start.1
  623.0 0.7 collective-permute-start
  643.7 15.7 %all-to-all-start.3 = ((bf16[32,64,128]{2,1,0:T(8,128)(2,1)}), bf16[32,64,128]{2,1,0:T(8,128)(2,1)S(1)}, u32[]{:S(2)}, u32[]{:S(2)}) async-start(bf16[32,64,128]{2,1,0:T(8,128)(2,1)} %bitcast.127), calls=%async_computation.3 | async-start | bytes 1048576 | tf_op jit(solution)/shard_map/while/body/eval_jaxpr/all_to_all | solution.py:168
  660.4 7.4 collective-permute-start.1
  703.7 0.7 collective-permute-start
  724.4 15.7 %all-to-all-start.3 = ((bf16[32,64,128]{2,1,0:T(8,128)(2,1)}), bf16[32,64,128]{2,1,0:T(8,128)(2,1)S(1)}, u32[]{:S(2)}, u32[]{:S(2)}) async-start(bf16[32,64,128]{2,1,0:T(8,128)(2,1)} %bitcast.127), calls=%async_computation.3 | async-start | bytes 1048576 | tf_op jit(solution)/shard_map/while/body/eval_jaxpr/all_to_all | solution.py:168
  741.1 7.4 collective-permute-start.1
  804.4 15.7 %all-to-all-start.16 = ((bf16[32,64,128]{2,1,0:T(8,128)(2,1)}), bf16[32,64,128]{2,1,0:T(8,128)(2,1)S(1)}, u32[]{:S(2)}, u32[]{:S(2)}) async-start(bf16[32,64,128]{2,1,0:T(8,128)(2,1)} %bitcast.63), calls=%async_computation.16 | async-start | bytes 1048576 | tf_op jit(solution)/shard_map/all_to_all | solution.py:168
  808.5 12.6 %collective-permute-start.10 = (bf16[2,16,16,128]{3,2,1,0:T(8,128)(2,1)S(1)}, bf16[2,16,16,128]{3,2,1,0:T(8,128)(2,1)S(1)}, u32[]{:S(2)}, u32[]{:S(2)}) collective-permute-start(bf16[2,16,16,128]{3,2,1,0:T(8,128)(2,1)S(1)} %slice_select_fusion.1), channel_id=1, source_target_pairs={{0,32},{32,0},{64,96},{96,64},{128,160},{160,128},{192,224},{224,1... | collective-permute-start | bytes 393224 | tf_op jit(solution)/shard_map/ppermute | solution.py:241
  (1 other events, 0.7 us)
